TPU v7x, 256 devices: a whole 4x4x8 slice. The times are simulated.
256 devices in a mesh: ctx: 128 (over x, z, y_lo, core), head: 2 (over y_hi).
Axes of the slice: x: 4, y: 4 (y_hi: 2, y_lo: 2; y = y_hi * 2 + y_lo), z: 8, core: 2. Of those that a mesh axis runs over, the one named last changes fastest.
Arguments:
- queries: bfloat16 [32768, 4096], P('ctx', 'head')
- keys: bfloat16 [32768, 256], P('ctx', 'head')
- values: bfloat16 [32768, 256], P('ctx', 'head'), may hold values from -6 to 6
- comp_keys: bfloat16 [512, 256], P('ctx', 'head')
- comp_values: bfloat16 [512, 256], P('ctx', 'head'), may hold values from -6 to 6
- selected: int32 [512, 15], replicated, may hold values from -1 to 507, as said below
- inputs: bfloat16 [32768, 2560], P('ctx'), may hold values from -6 to 6
- w_gate: bfloat16 [2560, 64], P(None, 'head'), may hold values from -0.125 to 0.125
- d_out: bfloat16 [32768, 4096], P('ctx', 'head'), may hold values from -6 to 6
Outputs:
- d_queries: bfloat16 [32768, 4096], P('ctx', 'head')
- d_keys: bfloat16 [32768, 256], P('ctx', 'head')
- d_values: bfloat16 [32768, 256], P('ctx', 'head')
- d_comp_keys: bfloat16 [512, 256], P('ctx', 'head')
- d_comp_values: bfloat16 [512, 256], P('ctx', 'head')
- d_inputs: bfloat16 [32768, 2560], P('ctx', 'head')
Inputs may be any that keep to these rules, and one draw needn't show every extreme that they name: `selected`: block c lies on index c // 4 of ctx. Let H = 128 // 2. Entry j of row b names a block on the index that lies r places before the index holding block b, where r = 1 + j * max(H - 1, 0) // 14 for even b and r = H + 1 + j * max(H - 2, 0) // 14 for odd b; the entry is -1 where that index would be below 0 or where r equals that of entry j - 1 of the same row. Over the 4 rows of one index of ctx, each index that is named is named exactly 2 times.
All inputs are finite; a program needn't handle non-finite values.
Results may differ from a plain program's by a relative error of at most 0.019.
Values may be sent and summed in bfloat16 or wider, within the bound.
A program may use at most 128 MiB of HBM per device.

v0:
```python
import jax
import jax.numpy as jnp
from jax import lax
from jax.sharding import PartitionSpec as P

BLK = 64
PICKS = 15


def attend(query_blk, key_set, value_set, visible, dout_blk, gate_blk):
    scale = key_set.shape[1] ** (-0.5)
    scores = (
        jnp.einsum("thd,kd->thk", query_blk, key_set, preferred_element_type=jnp.float32) * scale
    )
    scores = jnp.where(visible[:, None, :], scores, -jnp.inf)
    top = jnp.max(scores, axis=-1, keepdims=True)
    expo = jnp.exp(scores - top)
    probs = (expo / jnp.sum(expo, axis=-1, keepdims=True)).astype(jnp.bfloat16)
    out = jnp.einsum("thk,kd->thd", probs, value_set, preferred_element_type=jnp.float32)
    d_gate = jnp.sum(dout_blk.astype(jnp.float32) * out, axis=-1)
    d_branch = (gate_blk[:, :, None] * dout_blk.astype(jnp.float32)).astype(jnp.bfloat16)
    d_prob = jnp.einsum("thd,kd->thk", d_branch, value_set, preferred_element_type=jnp.float32)
    delta = jnp.sum(probs.astype(jnp.float32) * d_prob, axis=-1, keepdims=True)
    d_score = (probs.astype(jnp.float32) * (d_prob - delta) * scale).astype(jnp.bfloat16)
    d_query = jnp.einsum("thk,kd->thd", d_score, key_set, preferred_element_type=jnp.float32)
    d_key = jnp.einsum("thk,thd->kd", d_score, query_blk, preferred_element_type=jnp.float32)
    d_value = jnp.einsum("thk,thd->kd", probs, d_branch, preferred_element_type=jnp.float32)
    return (d_query, d_key, d_value, d_gate)


def body(queries, keys, values, comp_keys, comp_values, selected, inputs, w_gate, d_out):
    tokens_here = queries.shape[0]
    head_size = keys.shape[1]
    heads = queries.shape[1] // head_size
    blocks_here = tokens_here // BLK
    capacity = blocks_here // 2
    ranks = lax.axis_size("ctx")
    rank_here = lax.axis_index("ctx")
    all_blocks = blocks_here * ranks
    entries = blocks_here * PICKS
    gate = jax.nn.sigmoid(jnp.dot(inputs, w_gate, preferred_element_type=jnp.float32))
    all_ck, all_cv = (
        lax.all_gather(comp_keys, "ctx", axis=0, tiled=True),
        lax.all_gather(comp_values, "ctx", axis=0, tiled=True),
    )
    my_rows = lax.dynamic_slice_in_dim(selected, rank_here * blocks_here, blocks_here, 0).reshape(
        entries
    )
    valid = my_rows >= 0
    valid_rows = valid.reshape(blocks_here, PICKS)
    key_blocks = keys.reshape(blocks_here, BLK, head_size)
    value_blocks = values.reshape(blocks_here, BLK, head_size)
    owner = jnp.where(valid, my_rows // blocks_here, -1)
    order_ids = jnp.arange(entries, dtype=jnp.int32)
    earlier = (
        (owner[:, None] == owner[None, :])
        & (order_ids[None, :] < order_ids[:, None])
        & valid[None, :]
    )
    rank_mine = jnp.sum(earlier.astype(jnp.int32), axis=1)
    slot = jnp.where(valid, owner * capacity + rank_mine, ranks * capacity)
    table = selected.reshape(ranks, entries)
    asked = (table >= 0) & (table // blocks_here == rank_here)
    asked_rank = jnp.cumsum(asked.astype(jnp.int32), axis=1) - 1
    local_block = table % blocks_here
    hit = asked[:, :, None] & (
        asked_rank[:, :, None] == jnp.arange(capacity, dtype=jnp.int32)[None, None, :]
    )
    present = jnp.any(hit, axis=1)
    local_index = jnp.sum(jnp.where(hit, local_block[:, :, None], 0), axis=1)
    send_k = jnp.where(
        present[:, :, None, None], key_blocks[local_index], jnp.zeros((), jnp.bfloat16)
    )
    send_v = jnp.where(
        present[:, :, None, None], value_blocks[local_index], jnp.zeros((), jnp.bfloat16)
    )
    recv_k, recv_v = (
        lax.all_to_all(send_k, "ctx", split_axis=0, concat_axis=0, tiled=True),
        lax.all_to_all(send_v, "ctx", split_axis=0, concat_axis=0, tiled=True),
    )
    fetch_index = jnp.where(valid, slot, 0)
    fetch_k = recv_k.reshape(ranks * capacity, BLK, head_size)[fetch_index].reshape(
        blocks_here, PICKS, BLK, head_size
    )
    fetch_v = recv_v.reshape(ranks * capacity, BLK, head_size)[fetch_index].reshape(
        blocks_here, PICKS, BLK, head_size
    )
    lower = jnp.arange(BLK)[:, None] >= jnp.arange(BLK)[None, :]

    def step(carry, block):
        dck_acc, dcv_acc = carry
        query_blk = lax.dynamic_slice_in_dim(queries, block * BLK, BLK, 0).reshape(
            BLK, heads, head_size
        )
        dout_blk = lax.dynamic_slice_in_dim(d_out, block * BLK, BLK, 0).reshape(
            BLK, heads, head_size
        )
        gate_blk = lax.dynamic_slice_in_dim(gate, block * BLK, BLK, 0)
        pos = rank_here * tokens_here + block * BLK + jnp.arange(BLK, dtype=jnp.int32)
        vis_c = jnp.arange(all_blocks, dtype=jnp.int32)[None, :] * BLK <= pos[:, None]
        dqc, dckb, dcvb, dgc = attend(
            query_blk, all_ck, all_cv, vis_c, dout_blk, gate_blk[:, :heads]
        )
        own_k = lax.dynamic_slice_in_dim(keys, block * BLK, BLK, 0)
        own_v = lax.dynamic_slice_in_dim(values, block * BLK, BLK, 0)
        key_set = jnp.concatenate([own_k, fetch_k[block].reshape(PICKS * BLK, head_size)], axis=0)
        value_set = jnp.concatenate([own_v, fetch_v[block].reshape(PICKS * BLK, head_size)], axis=0)
        vis_p = jnp.broadcast_to(jnp.repeat(valid_rows[block], BLK)[None, :], (BLK, PICKS * BLK))
        vis_s = jnp.concatenate([lower, vis_p], axis=1)
        dqs, dks, dvs, dgs = attend(
            query_blk, key_set, value_set, vis_s, dout_blk, gate_blk[:, heads:]
        )
        d_query = (dqc + dqs).reshape(BLK, heads * head_size).astype(jnp.bfloat16)
        d_gate = jnp.concatenate([dgc, dgs], axis=-1)
        picks_k = dks[BLK:].reshape(PICKS, BLK, head_size)
        picks_v = dvs[BLK:].reshape(PICKS, BLK, head_size)
        return (
            (dck_acc + dckb, dcv_acc + dcvb),
            (d_query, d_gate, dks[:BLK], dvs[:BLK], picks_k, picks_v),
        )

    start = (
        jnp.zeros((all_blocks, head_size), jnp.float32),
        jnp.zeros((all_blocks, head_size), jnp.float32),
    )
    carry, outs = lax.scan(step, start, jnp.arange(blocks_here, dtype=jnp.int32))
    d_queries = outs[0].reshape(tokens_here, heads * head_size)
    d_gate = outs[1].reshape(tokens_here, 2 * heads)
    empty = jnp.zeros((ranks * capacity, BLK, head_size), jnp.float32)
    back_k = empty.at[slot].set(outs[4].reshape(entries, BLK, head_size), mode="drop")
    back_v = empty.at[slot].set(outs[5].reshape(entries, BLK, head_size), mode="drop")
    back_k = back_k.reshape(ranks, capacity, BLK, head_size)
    back_v = back_v.reshape(ranks, capacity, BLK, head_size)
    home_k, home_v = (
        lax.all_to_all(
            back_k.astype(jnp.bfloat16), "ctx", split_axis=0, concat_axis=0, tiled=True
        ).astype(back_k.dtype),
        lax.all_to_all(
            back_v.astype(jnp.bfloat16), "ctx", split_axis=0, concat_axis=0, tiled=True
        ).astype(back_v.dtype),
    )
    onehot = present[:, :, None] & (
        local_index[:, :, None] == jnp.arange(blocks_here, dtype=jnp.int32)[None, None, :]
    )
    onehot = onehot.astype(jnp.float32).reshape(ranks * capacity, blocks_here)
    sum_k = jnp.einsum(
        "nj,nx->jx",
        onehot,
        home_k.reshape(ranks * capacity, BLK * head_size),
        precision=lax.Precision.HIGHEST,
    )
    sum_v = jnp.einsum(
        "nj,nx->jx",
        onehot,
        home_v.reshape(ranks * capacity, BLK * head_size),
        precision=lax.Precision.HIGHEST,
    )
    d_keys = (
        outs[2].reshape(tokens_here, head_size) + sum_k.reshape(tokens_here, head_size)
    ).astype(jnp.bfloat16)
    d_values = (
        outs[3].reshape(tokens_here, head_size) + sum_v.reshape(tokens_here, head_size)
    ).astype(jnp.bfloat16)
    dck_sum, dcv_sum = (
        lax.psum_scatter(carry[0], "ctx", scatter_dimension=0, tiled=True),
        lax.psum_scatter(carry[1], "ctx", scatter_dimension=0, tiled=True),
    )
    d_z = (d_gate * gate * (1.0 - gate)).astype(jnp.bfloat16)
    partial_terms = lax.dot_general(
        d_z, w_gate, (((1,), (1,)), ((), ())), preferred_element_type=jnp.float32
    )
    d_inputs = lax.psum_scatter(
        partial_terms.astype(jnp.bfloat16), "head", scatter_dimension=1, tiled=True
    )
    return (
        d_queries,
        d_keys,
        d_values,
        dck_sum.astype(jnp.bfloat16),
        dcv_sum.astype(jnp.bfloat16),
        d_inputs,
    )


def solution(mesh):
    in_specs = (
        P("ctx", "head"),
        P("ctx", "head"),
        P("ctx", "head"),
        P("ctx", "head"),
        P("ctx", "head"),
        P(),
        P("ctx", None),
        P(None, "head"),
        P("ctx", "head"),
    )
    out_specs = (
        P("ctx", "head"),
        P("ctx", "head"),
        P("ctx", "head"),
        P("ctx", "head"),
        P("ctx", "head"),
        P("ctx", "head"),
    )
    return jax.shard_map(body, mesh=mesh, in_specs=in_specs, out_specs=out_specs, check_vma=False)
```

profile of v0, /device:TPU:33, one launch (start us, length us, event | category | flops | bytes accessed | tf_op | source)
XLA Modules:
  0.0 1534.9 jit_solution(11870989608007843724)
XLA Ops:
  9.6 3.1 gather_fusion.2
  12.7 3.0 gather_fusion
  15.9 5.1 broadcast_select_fusion
  21.0 109.0 %all_to_all.20 = bf16[128,2,64,128]{3,2,1,0:T(8,128)(2,1)} all-to-all(bf16[128,2,64,128]{3,2,1,0:T(8,128)(2,1)S(1)} %get-tuple-element.484), channel_id=1, replica_groups=mesh['ctx'=128,'head'=2] {'ctx'}, dimensions={0} | all-to-all | bytes 8388608 | tf_op jit(solution)/shard_map/all_to_all | solution.py:78
  130.0 9.5 all-to-all-start.1
  139.7 243.0 %all-gather = bf16[128,4,128]{2,1,0:T(4,128)(2,1)} all-gather(bf16[1,4,128]{2,1,0:T(4,128)(2,1)S(1)} %bitcast.225), channel_id=1, replica_groups=mesh['ctx'=128,'head'=2] {'ctx'}, dimensions={0}, use_global_device_ids=true | all-gather | bytes 132096 | tf_op jit(solution)/shard_map/all_gather | solution.py:43
  382.7 162.6 %all-gather.1 = bf16[128,4,128]{2,1,0:T(4,128)(2,1)} all-gather(bf16[1,4,128]{2,1,0:T(4,128)(2,1)S(1)} %bitcast.226), channel_id=1, replica_groups=mesh['ctx'=128,'head'=2] {'ctx'}, dimensions={0}, use_global_device_ids=true | all-gather | bytes 132096 | tf_op jit(solution)/shard_map/all_gather | solution.py:44
  547.2 3.8 gather_fusion.1
  551.0 3.9 gather_fusion.3
  554.9 209.9 %while.27 = (s32[]{:T(128)}, f32[512,128]{1,0:T(8,128)}, f32[512,128]{1,0:T(8,128)}, bf16[4,64,2048]{2,1,0:T(8,128)(2,1)}, f32[4,64,32]{2,1,0:T(8,128)}, /*index...) while((s32[]{:T(128)}, f32[512,128]{1,0:T(8,128)}, ...), condition=%wide.region_13.14_spmd.clone, body=%wide.region_4.13_spmd.clone.sunk | while | flops 2451813376 | bytes 84646016 | solution.py:126
  560.7 4.0 fusion.162
  564.7 2.7 divide_convert_fusion.5
  568.5 2.7 fusion.163
  571.2 5.6 fusion.169
  581.1 3.1 fusion.156
  584.2 1.8 divide_convert_fusion.4
  587.3 5.8 fusion.164
  593.1 1.8 fusion.158
  595.0 2.9 fusion.165
  598.7 2.6 convolution_bitcast_fusion.4
  602.9 3.1 fusion.159
  613.2 4.0 fusion.162
  617.2 2.7 divide_convert_fusion.5
  621.0 2.7 fusion.163
  623.7 5.6 fusion.169
  633.6 3.1 fusion.156
  636.7 1.8 divide_convert_fusion.4
  639.8 5.8 fusion.164
  645.6 1.8 fusion.158
  647.5 2.9 fusion.165
  651.2 2.6 convolution_bitcast_fusion.4
  655.4 3.1 fusion.159
  665.7 4.0 fusion.162
  669.7 2.7 divide_convert_fusion.5
  673.5 2.7 fusion.163
  676.2 5.6 fusion.169
  686.1 3.1 fusion.156
  689.1 1.8 divide_convert_fusion.4
  692.2 5.8 fusion.164
  699.9 2.9 fusion.165
  703.7 2.6 convolution_bitcast_fusion.4
  707.8 3.1 fusion.159
  718.2 4.0 fusion.162
  722.2 2.7 divide_convert_fusion.5
  726.0 2.7 fusion.163
  728.7 5.6 fusion.169
  738.5 3.1 fusion.156
  741.6 1.8 divide_convert_fusion.4
  744.7 5.8 fusion.164
  752.4 2.9 fusion.165
  756.1 2.6 convolution_bitcast_fusion.4
  760.2 3.1 fusion.159
  764.8 4.3 broadcast_in_dim.163.clone.1
  769.1 8.5 scatter_fusion.1
  777.6 6.4 convert_element_type.116
  784.0 10.0 all-to-all-start.3
  794.0 4.3 broadcast_in_dim.163.clone
  798.3 8.5 scatter_fusion
  806.8 6.4 convert_element_type.113
  813.2 75.9 %all-to-all-done.3 = bf16[128,2,64,128]{3,2,1,0:T(8,128)(2,1)} async-done(((bf16[128,2,64,128]{3,2,1,0:T(8,128)(2,1)}), bf16[128,2,64,128]{3,2,1,0:T(8,128)(2,1)}, u32[]{:S(2)}, u32[]{:S(2)}) %all-to-all-start.3) | async-done | bytes 4194336 | tf_op jit(solution)/shard_map/all_to_all | solution.py:138
  889.1 9.5 all-to-all-start.2
  902.2 614.0 %all-reduce.4 = (bf16[512,128]{1,0:T(8,128)(2,1)S(1)}, bf16[512,128]{1,0:T(8,128)(2,1)S(1)}) all-reduce(f32[512,128]{1,0:T(8,128)S(1)} %copy-done.22, f32[512,128]{1,0:T(8,128)S(1)} %copy-done.25), channel_id=2, replica_groups=mesh['ctx'=128,'head'=2] {'ctx'}, use_global_device_ids=true, to_apply=%region_16.17.clone | all-reduce | flops 131072 | bytes 786432
  1517.3 4.5 fusion.67
  1522.0 4.7 fusion.70
  (343 shorter events, 67.2 us)
Async XLA Ops:
  7.2 538.9 %copy-start = (bf16[256,2560]{1,0:T(8,128)(2,1)S(1)}, bf16[256,2560]{1,0:T(8,128)(2,1)}, u32[]{:S(2)}) copy-start(bf16[256,2560]{1,0:T(8,128)(2,1)} %param.17) | copy-start | bytes 3932164
  9.6 3.1 copy-start.2
  15.9 5.1 copy-start.26
  130.0 9.8 copy-start.35
  130.0 252.7 %copy-start.36 = (bf16[4,128]{1,0:T(4,128)(2,1)S(1)}, bf16[4,128]{1,0:T(4,128)(2,1)}, u32[]{:S(2)}) copy-start(bf16[4,128]{1,0:T(4,128)(2,1)} %param.15) | copy-start | bytes 3076
  130.0 416.1 %copy-start.16 = (bf16[2560,32]{0,1:T(8,128)(2,1)S(1)}, bf16[2560,32]{0,1:T(8,128)(2,1)}, u32[]{:S(2)}) copy-start(bf16[2560,32]{0,1:T(8,128)(2,1)} %param.18) | copy-start | bytes 491524
  130.0 421.0 %all-to-all-start.1 = ((bf16[128,2,64,128]{3,2,1,0:T(8,128)(2,1)}), bf16[128,2,64,128]{3,2,1,0:T(8,128)(2,1)}, u32[]{:S(2)}, u32[]{:S(2)}) async-start(bf16[128,2,64,128]{3,2,1,0:T(8,128)(2,1)} %get-tuple-element.483), calls=%async_computation.1 | async-start | bytes 8388608 | tf_op jit(solution)/shard_map/all_to_all | solution.py:79
  557.3 7.4 copy-start.6
  557.3 7.4 copy-start.18
  560.4 4.3 copy-start.9
  567.5 12.7 copy-start.4
  584.2 3.1 copy-start.10
  584.2 3.1 copy-start.19
  595.0 3.8 copy-start.12
  598.7 4.2 copy-start.8
  598.7 4.2 copy-start.20
  602.9 3.1 copy-start.23
  609.8 7.4 copy-start.6
  609.8 7.4 copy-start.18
  612.9 4.3 copy-start.9
  620.0 12.7 copy-start.4
  621.0 2.7 copy-start.7
  636.7 3.1 copy-start.10
  636.7 3.1 copy-start.19
  647.5 3.8 copy-start.12
  651.2 4.1 copy-start.8
  651.2 4.1 copy-start.20
  655.4 3.1 copy-start.23
  662.3 7.4 copy-start.6
  662.3 7.4 copy-start.18
  665.4 4.3 copy-start.9
  672.5 12.7 copy-start.4
  673.5 2.7 copy-start.7
  689.1 3.1 copy-start.10
  689.1 3.1 copy-start.19
  699.9 3.8 copy-start.12
  703.7 4.1 copy-start.8
  703.7 4.1 copy-start.20
  707.8 3.1 copy-start.23
  714.7 7.4 copy-start.6
  714.8 7.4 copy-start.18
  717.8 4.3 copy-start.9
  724.9 12.7 copy-start.4
  726.0 2.7 copy-start.7
  741.6 3.1 copy-start.10
  741.6 3.1 copy-start.19
  752.4 3.8 copy-start.12
  756.1 4.1 copy-start.8
  756.1 4.1 copy-start.20
  760.2 3.1 copy-start.23
  764.8 4.3 copy-start.14
  764.8 4.3 copy-start.34
  784.0 105.1 %all-to-all-start.3 = ((bf16[128,2,64,128]{3,2,1,0:T(8,128)(2,1)}), bf16[128,2,64,128]{3,2,1,0:T(8,128)(2,1)}, u32[]{:S(2)}, u32[]{:S(2)}) async-start(bf16[128,2,64,128]{3,2,1,0:T(8,128)(2,1)} %bitcast.210), calls=%async_computation.3 | async-start | bytes 8388608 | tf_op jit(solution)/shard_map/all_to_all | solution.py:138
  794.0 4.3 copy-start.13
  889.1 9.6 copy-start.28
  889.1 9.7 copy-start.15
  889.1 9.7 copy-start.17
  889.1 632.8 %all-to-all-start.2 = ((bf16[128,2,64,128]{3,2,1,0:T(8,128)(2,1)}), bf16[128,2,64,128]{3,2,1,0:T(8,128)(2,1)}, u32[]{:S(2)}, u32[]{:S(2)}) async-start(bf16[128,2,64,128]{3,2,1,0:T(8,128)(2,1)} %bitcast.209), calls=%async_computation.2 | async-start | bytes 8388608 | tf_op jit(solution)/shard_map/all_to_all | solution.py:135
  898.7 3.5 copy-start.22
  898.7 3.5 copy-start.25
  898.7 629.4 %reduce-scatter.2.cloned.1.call-start = ((), (), s32[]{:S(2)}) async-start(), calls=%async_computation.5 | async-start | bytes 1966080 | tf_op jit(solution)/shard_map/reduce_scatter | solution.py:172
  1522.0 6.1 copy-start.1
  1522.0 4.8 copy-start.31
  1522.0 5.4 copy-start.30
  (26 other events, 43.5 us)
Sparse Core Ops, SparseCore 0:
  902.6 40.5 reduce-scatter.1
where the time goes:
time: 1550 us; the launch traced here: 1530 us
  blocking collectives  1130 us (73%)
  matrix products  146 us (9%)
  local copies, waits for them, and re-layouts  82.2 us (5%)
  waiting for transfers between devices  75.9 us (5%)
  other arithmetic  46.3 us (3%)
  starting transfers between devices  29.1 us (2%)
    unnamed x1, blocking collectives  614 us
    all_gather x1, blocking collectives, body(): lax.all_gather(comp_keys, 'ctx', axis=0, tiled=True)  243 us
    all_gather x1, blocking collectives, body(): lax.all_gather(comp_values, 'ctx', axis=0, tiled=True)  163 us
    all_to_all x1, blocking collectives, body(): lax.all_to_all(send_k, 'ctx', split_axis=0, concat_axis=0, tiled=True)  109 us
    all_to_all x1, waiting for transfers between devices, body(): lax.all_to_all(back_v.astype(jnp.bfloat16), 'ctx', split_axis=0, concat_a...  75.9 us
    dot_general x8, matrix products, attend(): jnp.einsum('thk,thd->kd', d_score, query_blk, preferred_element_type=jnp....  34.9 us
    dot_general x8, matrix products, attend(): jnp.einsum('thk,kd->thd', d_score, key_set, preferred_element_type=jnp.fl...  34.6 us
  transfers between devices with their start and end apart: 4, of which 1 were waited for; matrix products, arithmetic and copies ran while one was open for 3% of the time, Pallas kernels for 0%

commit v1 on v0

v1 whole, which is shorter than its diff:
```python
import functools

import jax
import jax.numpy as jnp
from jax import lax
from jax.experimental import pallas as pl
from jax.experimental.pallas import tpu as pltpu
from jax.sharding import PartitionSpec as P

BLK = 64
PICKS = 15
HD = 128
QB = 4
RANKS = 128
HEADS = 16
LOW = 16
OUTER = RANKS // LOW
HALF = RANKS // 2
SCALE = HD ** -0.5
LOG2E = 1.4426950408889634
BF = jnp.bfloat16
F32 = jnp.float32
MIB = 1 << 20


def reach(parity, j):
    if parity == 0:
        return 1 + (j * (HALF - 1)) // (PICKS - 1)
    return HALF + 1 + (j * (HALF - 2)) // (PICKS - 1)


REACH = [(p, j, reach(p, j)) for p in range(2) for j in range(PICKS)]


def count(conditions):
    return sum(c.astype(jnp.int32) for c in conditions)


def at_ctx(index):
    return {"ctx": index}


def signal(sem, device):
    pl.semaphore_signal(sem, inc=1, device_id=device, device_id_type=pl.DeviceIdType.MESH)


def remote(src, dst, send_sem, recv_sem, device):
    return pltpu.make_async_remote_copy(
        src_ref=src,
        dst_ref=dst,
        send_sem=send_sem,
        recv_sem=recv_sem,
        device_id=device,
        device_id_type=pl.DeviceIdType.MESH,
    )


def fetch_kernel(
    sel_ref, k_ref, v_ref, ck_ref, cv_ref, w_ref,
    kv_ref, comp_ref, wother_ref,
    out_buf, kv_send, kv_recv, a_send, a_recv, b_send, b_recv, w_sems,
):
    me = lax.axis_index("ctx")
    hd = lax.axis_index("head")
    group = me // LOW
    low = me % LOW
    partner = {"head": 1 - hd}

    barrier = pltpu.get_barrier_semaphore()
    for a in range(LOW):
        @pl.when(a != low)
        def _():
            signal(barrier, at_ctx(group * LOW + a))
    for p, j, r in REACH:
        @pl.when(me >= r)
        def _():
            signal(barrier, at_ctx(me - r))
    for g in range(OUTER):
        @pl.when(g < group)
        def _():
            signal(barrier, at_ctx(g * LOW + low))
    signal(barrier, partner)

    comp_ref[pl.ds(me, 1), 0:4, :] = ck_ref[...].astype(F32)[None]
    comp_ref[pl.ds(me, 1), 4:8, :] = cv_ref[...].astype(F32)[None]
    for g in range(OUTER):
        @pl.when(g > group)
        def _():
            comp_ref[g * LOW:(g + 1) * LOW] = jnp.zeros((LOW, 8, HD), F32)
    for p, j, r in REACH:
        slot = p * PICKS + j
        asker = jnp.minimum(me + r, RANKS - 1)
        for i in range(2):
            local = sel_ref[(asker * QB + p + 2 * i) * PICKS + j] & (QB - 1)
            out_buf[slot, i, :, 0:HD] = k_ref[local]
            out_buf[slot, i, :, HD:] = v_ref[local]
        @pl.when(me < r)
        def _():
            kv_ref[:, p, j] = jnp.zeros((2, BLK, 2 * HD), BF)
    for b in range(QB):
        kv_ref[b // 2, b % 2, PICKS, :, 0:HD] = k_ref[b]
        kv_ref[b // 2, b % 2, PICKS, :, HD:] = v_ref[b]

    askers = count([me + r < RANKS for _, _, r in REACH])
    pl.semaphore_wait(barrier, askers + (LOW - 1) + (OUTER - 1 - group) + 1)

    def a_copy(a, slot):
        return remote(
            comp_ref.at[slot], comp_ref.at[slot], a_send.at[a], a_recv.at[slot % LOW],
            at_ctx(group * LOW + a),
        )

    def kv_copy(p, j, r, target):
        slot = p * PICKS + j
        return remote(
            out_buf.at[slot], kv_ref.at[:, p, j], kv_send.at[slot], kv_recv.at[slot],
            at_ctx(target),
        )

    def b_copy(g, source):
        rows = pl.ds(source * LOW, LOW)
        return remote(
            comp_ref.at[rows], comp_ref.at[rows], b_send.at[g], b_recv.at[source],
            at_ctx(g * LOW + low),
        )

    w_copy = remote(w_ref.at[1 - hd], wother_ref, w_sems.at[0], w_sems.at[1], partner)

    for a in range(LOW):
        @pl.when(a != low)
        def _():
            a_copy(a, me).start()
    for p, j, r in REACH:
        @pl.when(me + r < RANKS)
        def _():
            kv_copy(p, j, r, me + r).start()
    w_copy.start()
    for a in range(LOW):
        @pl.when(a != low)
        def _():
            a_copy(a, group * LOW + a).wait_recv()
    for g in range(OUTER):
        @pl.when(g > group)
        def _():
            b_copy(g, group).start()
    for g in range(OUTER):
        @pl.when(g < group)
        def _():
            b_copy(g, g).wait_recv()
    for p, j, r in REACH:
        @pl.when(me >= r)
        def _():
            kv_copy(p, j, r, me - r).wait_recv()
    w_copy.wait_recv()
    for a in range(LOW):
        @pl.when(a != low)
        def _():
            a_copy(a, me).wait_send()
    for p, j, r in REACH:
        @pl.when(me + r < RANKS)
        def _():
            kv_copy(p, j, r, me + r).wait_send()
    for g in range(OUTER):
        @pl.when(g > group)
        def _():
            b_copy(g, group).wait_send()
    w_copy.wait_send()


def nt(a, b):
    return lax.dot_general(a, b, (((1,), (1,)), ((), ())), preferred_element_type=F32)


def nn(a, b):
    return lax.dot_general(a, b, (((1,), (0,)), ((), ())), preferred_element_type=F32)


def scores_backward(k, v, kt, bias, q, do):
    s = nt(k, q) * (SCALE * LOG2E) + bias
    top = jnp.max(s, axis=0, keepdims=True)
    e = jnp.exp2(s - top)
    prob = e * (1.0 / jnp.sum(e, axis=0, keepdims=True))
    dp = nt(v, do)
    delta = jnp.sum(prob * dp, axis=0, keepdims=True)
    ds = (prob * (dp - delta)).astype(BF)
    dv = nn(prob.astype(BF), do)
    dk = nn(ds, q)
    dqt = nn(kt, ds)
    return dqt, dk, dv, delta


def local_kernel(
    q_ref, do_ref, x_ref, w_ref, kv_ref, comp_ref,
    dq_ref, dkv_ref, down_ref, dcomp_ref, dz_ref,
    doc, dos, dq_acc, bias_c, bias_s, ck, cv, ckt, kt, dc_acc, dkv_acc, delta_c, delta_s,
):
    me = lax.axis_index("ctx")
    tokens = q_ref.shape[0]
    half = w_ref.shape[2]

    x0, x1 = x_ref[:, 0:half], x_ref[:, half:]
    gate = jax.nn.sigmoid(nt(x0, w_ref[0]) + nt(x1, w_ref[1]))
    for h in range(HEADS):
        slab = do_ref[:, h * HD:(h + 1) * HD].astype(F32)
        doc[:, h * HD:(h + 1) * HD] = (gate[:, h:h + 1] * slab).astype(BF)
        dos[:, h * HD:(h + 1) * HD] = (gate[:, HEADS + h:HEADS + h + 1] * slab).astype(BF)

    pairs = comp_ref[...].reshape(RANKS // 2, 2, 8, HD)
    even, odd = pairs[:, 0], pairs[:, 1]
    top_rows = lax.broadcasted_iota(jnp.int32, (RANKS // 2, 8, HD), 1) < 4
    swap = lambda z: pltpu.roll(z, 4, 1)
    keys_c = jnp.where(top_rows, even, swap(odd)).reshape(RANKS * 4, HD)
    vals_c = jnp.where(top_rows, swap(even), odd).reshape(RANKS * 4, HD)
    ck[...] = keys_c.astype(BF)
    cv[...] = vals_c.astype(BF)
    ckt[...] = keys_c.T.astype(BF)

    row = lax.broadcasted_iota(jnp.int32, (RANKS * QB, tokens), 0)
    col = lax.broadcasted_iota(jnp.int32, (RANKS * QB, tokens), 1)
    bias_c[...] = jnp.where(row <= me * QB + col // BLK, 0.0, -jnp.inf)
    srow = lax.broadcasted_iota(jnp.int32, (BLK, 4 * BLK), 0)
    scol = lax.broadcasted_iota(jnp.int32, (BLK, 4 * BLK), 1) % BLK
    own_bias = jnp.where(srow <= scol, 0.0, -jnp.inf)
    for p, j, r in REACH:
        bias_s[p, j * BLK:(j + 1) * BLK, :] = jnp.full(
            (BLK, 4 * BLK), jnp.where(me >= r, 0.0, -jnp.inf), F32
        )
    for p in range(2):
        bias_s[p, PICKS * BLK:, :] = own_bias

    dc_acc[...] = jnp.zeros_like(dc_acc)

    def comp_head(h, carry):
        lanes = pl.ds(pl.multiple_of(h * HD, HD), HD)
        dqt, dk, dv, delta = scores_backward(
            ck[...], cv[...], ckt[...], bias_c[...], q_ref[:, lanes], doc[:, lanes]
        )
        dq_acc[:, lanes] = dqt.T
        dc_acc[0] += dk
        dc_acc[1] += dv
        delta_c[pl.ds(h, 1), :] = delta
        return carry

    lax.fori_loop(0, HEADS, comp_head, 0)

    def sel_block(b, carry):
        rows = pl.ds(pl.multiple_of(b * BLK, BLK), BLK)
        kt[...] = kv_ref[b, :, 0:HD].astype(F32).T.astype(BF)
        dkv_acc[...] = jnp.zeros_like(dkv_acc)
        bias = bias_s.at[lax.rem(b, 2)]

        def heads4(g, inner):
            lanes = [pl.ds(pl.multiple_of((g + 4 * i) * HD, HD), HD) for i in range(4)]
            q = jnp.concatenate([q_ref[rows, l] for l in lanes], axis=0)
            do = jnp.concatenate([dos[rows, l] for l in lanes], axis=0)
            dqt, dk, dv, delta = scores_backward(
                kv_ref[b, :, 0:HD], kv_ref[b, :, HD:], kt[...], bias[...], q, do
            )
            dq = dqt.T
            for i in range(4):
                total = (dq[i * BLK:(i + 1) * BLK] + dq_acc[rows, lanes[i]]) * SCALE
                dq_ref[rows, lanes[i]] = total.astype(BF)
            dkv_acc[:, 0:HD] += dk
            dkv_acc[:, HD:] += dv
            delta_s[b, pl.ds(g, 1), :] = delta
            return inner

        lax.fori_loop(0, 4, heads4, 0)
        factor = jnp.where(
            lax.broadcasted_iota(jnp.int32, (1, 2 * HD), 1) < HD, jnp.float32(SCALE), 1.0
        )
        dkv_ref[b] = (dkv_acc[...] * factor).astype(BF)
        down_ref[b] = dkv_acc[PICKS * BLK:, :] * factor
        return carry

    lax.fori_loop(0, QB, sel_block, 0)

    dck = (dc_acc[0] * SCALE).reshape(RANKS // 2, 8, HD)
    dcv = dc_acc[1].reshape(RANKS // 2, 8, HD)
    dcomp_ref[:, 0] = jnp.where(top_rows, dck, swap(dcv))
    dcomp_ref[:, 1] = jnp.where(top_rows, swap(dck), dcv)

    gate_t = jax.nn.sigmoid(nt(w_ref[0], x0) + nt(w_ref[1], x1))
    dz_ref[0:HEADS, :] = (delta_c[...] * (1.0 - gate_t[0:HEADS])).astype(BF)
    columns = []
    for b in range(QB):
        columns.append(
            jnp.concatenate([delta_s[b, :, i * BLK:(i + 1) * BLK] for i in range(4)], axis=0)
        )
    sel = jnp.concatenate(columns, axis=1)
    dz_ref[HEADS:, :] = (sel * (1.0 - gate_t[HEADS:])).astype(BF)


def return_kernel(
    dkv_ref, dcomp_ref, dz_ref,
    back_ref, csum_ref, dzother_ref,
    b_buf, b_sum, a_buf, kv_send, kv_recv, b_send, b_recv, a_send, a_recv, z_sems,
):
    me = lax.axis_index("ctx")
    hd = lax.axis_index("head")
    group = me // LOW
    low = me % LOW
    partner = {"head": 1 - hd}

    barrier = pltpu.get_barrier_semaphore()
    for g in range(OUTER):
        @pl.when(g > group)
        def _():
            signal(barrier, at_ctx(g * LOW + low))
    for p, j, r in REACH:
        @pl.when(me + r < RANKS)
        def _():
            signal(barrier, at_ctx(me + r))
    for a in range(LOW):
        @pl.when(a != low)
        def _():
            signal(barrier, at_ctx(group * LOW + a))
    signal(barrier, partner)
    owners = count([me >= r for _, _, r in REACH])
    pl.semaphore_wait(barrier, owners + group + (LOW - 1) + 1)

    def kv_copy(p, j, target):
        slot = p * PICKS + j
        return remote(
            dkv_ref.at[:, p, j], back_ref.at[slot], kv_send.at[slot], kv_recv.at[slot],
            at_ctx(target),
        )

    def b_copy(g, source):
        return remote(
            dcomp_ref.at[pl.ds(g * LOW, LOW)], b_buf.at[source], b_send.at[g], b_recv.at[source],
            at_ctx(g * LOW + low),
        )

    def a_copy(a, source):
        return remote(
            b_sum.at[a], a_buf.at[source], a_send.at[a], a_recv.at[source],
            at_ctx(group * LOW + a),
        )

    z_copy = remote(dz_ref, dzother_ref, z_sems.at[0], z_sems.at[1], partner)

    for g in range(OUTER):
        @pl.when(g < group)
        def _():
            b_copy(g, group).start()
    for p, j, r in REACH:
        @pl.when(me >= r)
        def _():
            kv_copy(p, j, me - r).start()
    z_copy.start()
    b_sum[...] = dcomp_ref[pl.ds(group * LOW, LOW)]
    for g in range(OUTER):
        @pl.when(g > group)
        def _():
            b_copy(g, g).wait_recv()
            b_sum[...] += b_buf[g]
    for a in range(LOW):
        @pl.when(a != low)
        def _():
            a_copy(a, low).start()
    a_buf[pl.ds(low, 1)] = b_sum[pl.ds(low, 1)]
    for a in range(LOW):
        @pl.when(a != low)
        def _():
            a_copy(a, a).wait_recv()
    csum_ref[...] = jnp.sum(a_buf[...], axis=0)
    z_copy.wait_recv()
    for p, j, r in REACH:
        @pl.when(me + r < RANKS)
        def _():
            kv_copy(p, j, me + r).wait_recv()
    for g in range(OUTER):
        @pl.when(g < group)
        def _():
            b_copy(g, group).wait_send()
    for p, j, r in REACH:
        @pl.when(me >= r)
        def _():
            kv_copy(p, j, me - r).wait_send()
    for a in range(LOW):
        @pl.when(a != low)
        def _():
            a_copy(a, low).wait_send()
    z_copy.wait_send()


def finish_kernel(
    sel_ref, back_ref, down_ref, csum_ref, dz_ref, dzother_ref, w_ref, wother_ref,
    dk_ref, dv_ref, dck_ref, dcv_ref, dx_ref, acc,
):
    me = lax.axis_index("ctx")
    hd = lax.axis_index("head")
    acc[...] = down_ref[...]
    for p, j, r in REACH:
        @pl.when(me + r < RANKS)
        def _():
            for i in range(2):
                local = sel_ref[((me + r) * QB + p + 2 * i) * PICKS + j] & (QB - 1)
                acc[local] += back_ref[p * PICKS + j, i].astype(F32)
    for b in range(QB):
        dk_ref[b * BLK:(b + 1) * BLK, :] = acc[b, :, 0:HD].astype(BF)
        dv_ref[b * BLK:(b + 1) * BLK, :] = acc[b, :, HD:].astype(BF)
    dck_ref[...] = csum_ref[0:4, :].astype(BF)
    dcv_ref[...] = csum_ref[4:8, :].astype(BF)
    mine = lax.dot_general(
        dz_ref[...], w_ref[hd], (((0,), (0,)), ((), ())), preferred_element_type=F32
    )
    other = lax.dot_general(
        dzother_ref[...], wother_ref[...], (((0,), (0,)), ((), ())), preferred_element_type=F32
    )
    dx_ref[...] = (mine + other).astype(BF)


VM = pl.BlockSpec(memory_space=pltpu.VMEM)
SM = pl.BlockSpec(memory_space=pltpu.SMEM)


def body(queries, keys, values, comp_keys, comp_values, selected, inputs, w_gate, d_out):
    tokens = queries.shape[0]
    width = inputs.shape[1]
    half = width // 2
    dma = lambda n: pltpu.SemaphoreType.DMA((n,))
    sel = selected.reshape(-1)
    w2 = w_gate.T.reshape(2 * HEADS, 2, half).transpose(1, 0, 2)
    slots = 2 * PICKS

    kv, comp, w_other = pl.pallas_call(
        fetch_kernel,
        name="fetch",
        out_shape=(
            jax.ShapeDtypeStruct((2, 2, PICKS + 1, BLK, 2 * HD), BF),
            jax.ShapeDtypeStruct((RANKS, 8, HD), F32),
            jax.ShapeDtypeStruct((2 * HEADS, half), BF),
        ),
        in_specs=[SM] + [VM] * 5,
        out_specs=(VM,) * 3,
        scratch_shapes=[
            pltpu.VMEM((slots, 2, BLK, 2 * HD), BF),
            dma(slots), dma(slots), dma(LOW), dma(LOW), dma(OUTER), dma(OUTER), dma(2),
        ],
        compiler_params=pltpu.CompilerParams(
            collective_id=0, has_side_effects=True, vmem_limit_bytes=16 * MIB
        ),
    )(sel, keys.reshape(QB, BLK, HD), values.reshape(QB, BLK, HD), comp_keys, comp_values, w2)

    keys_all = (PICKS + 1) * BLK
    dq, dkv, down, dcomp, dz = pl.pallas_call(
        local_kernel,
        name="local",
        out_shape=(
            jax.ShapeDtypeStruct(queries.shape, BF),
            jax.ShapeDtypeStruct((QB, keys_all, 2 * HD), BF),
            jax.ShapeDtypeStruct((QB, BLK, 2 * HD), F32),
            jax.ShapeDtypeStruct((RANKS // 2, 2, 8, HD), F32),
            jax.ShapeDtypeStruct((2 * HEADS, tokens), BF),
        ),
        in_specs=[VM] * 6,
        out_specs=(VM,) * 5,
        scratch_shapes=[
            pltpu.VMEM(queries.shape, BF),
            pltpu.VMEM(queries.shape, BF),
            pltpu.VMEM(queries.shape, F32),
            pltpu.VMEM((RANKS * QB, tokens), F32),
            pltpu.VMEM((2, keys_all, 4 * BLK), F32),
            pltpu.VMEM((RANKS * QB, HD), BF),
            pltpu.VMEM((RANKS * QB, HD), BF),
            pltpu.VMEM((HD, RANKS * QB), BF),
            pltpu.VMEM((HD, keys_all), BF),
            pltpu.VMEM((2, RANKS * QB, HD), F32),
            pltpu.VMEM((keys_all, 2 * HD), F32),
            pltpu.VMEM((HEADS, tokens), F32),
            pltpu.VMEM((QB, 4, 4 * BLK), F32),
        ],
        compiler_params=pltpu.CompilerParams(vmem_limit_bytes=48 * MIB),
    )(queries, d_out, inputs, w2, kv.reshape(QB, keys_all, 2 * HD), comp)

    back, csum, dz_other = pl.pallas_call(
        return_kernel,
        name="back",
        out_shape=(
            jax.ShapeDtypeStruct((slots, 2, BLK, 2 * HD), BF),
            jax.ShapeDtypeStruct((8, HD), F32),
            jax.ShapeDtypeStruct((2 * HEADS, tokens), BF),
        ),
        in_specs=[VM] * 3,
        out_specs=(VM,) * 3,
        scratch_shapes=[
            pltpu.VMEM((OUTER, LOW, 8, HD), F32),
            pltpu.VMEM((LOW, 8, HD), F32),
            pltpu.VMEM((LOW, 8, HD), F32),
            dma(slots), dma(slots), dma(OUTER), dma(OUTER), dma(LOW), dma(LOW), dma(2),
        ],
        compiler_params=pltpu.CompilerParams(
            collective_id=1, has_side_effects=True, vmem_limit_bytes=16 * MIB
        ),
    )(dkv.reshape(2, 2, PICKS + 1, BLK, 2 * HD), dcomp.reshape(RANKS, 8, HD), dz)

    dk, dv, dck, dcv, dx = pl.pallas_call(
        finish_kernel,
        name="finish",
        out_shape=(
            jax.ShapeDtypeStruct((tokens, HD), BF),
            jax.ShapeDtypeStruct((tokens, HD), BF),
            jax.ShapeDtypeStruct((QB, HD), BF),
            jax.ShapeDtypeStruct((QB, HD), BF),
            jax.ShapeDtypeStruct((tokens, half), BF),
        ),
        in_specs=[SM] + [VM] * 7,
        out_specs=(VM,) * 5,
        scratch_shapes=[pltpu.VMEM((QB, BLK, 2 * HD), F32)],
        compiler_params=pltpu.CompilerParams(vmem_limit_bytes=24 * MIB),
    )(sel, back, down, csum, dz, dz_other, w2, w_other)
    return dq, dk, dv, dck, dcv, dx


def solution(mesh):
    split = P("ctx", "head")
    in_specs = (split, split, split, split, split, P(), P("ctx", None), P(None, "head"), split)
    return jax.shard_map(body, mesh=mesh, in_specs=in_specs, out_specs=(split,) * 6, check_vma=False)
```

time: 1550 us -> 193 us (0.12)
  blocking collectives: 1130 us -> 0 us
  Pallas kernels: 0 us -> 180 us
  matrix products: 146 us -> 0 us
  waiting for transfers between devices: 75.9 us -> 0 us
  local copies, waits for them, and re-layouts: 82.2 us -> 11.7 us
  other arithmetic: 46.3 us -> 0 us
  starting transfers between devices: 29.1 us -> 0 us
    unnamed x1 -> x0, blocking collectives: 614 us -> none
    all_gather x2 -> x0, blocking collectives: 406 us -> none  [the longest x1 243 us: body(): lax.all_gather(comp_keys, 'ctx', axis=0, tiled=True)]
    pallas_call x0 -> x4, Pallas kernels: none -> 180 us  [the longest x1 72.2 us: body(): pl.pallas_call(return_kernel, name='back', out_shape=(jax.ShapeDtypeStruc...]
    dot_general x44 -> x0, matrix products: 118 us -> none  [the longest x8 34.9 us: attend(): jnp.einsum('thk,thd->kd', d_score, query_blk, preferred_element_type=jnp....]
    all_to_all x1 -> x0, blocking collectives: 109 us -> none  [body(): lax.all_to_all(send_k, 'ctx', split_axis=0, concat_axis=0, tiled=True)]
    all_to_all x3 -> x0, waiting for transfers between devices: 75.9 us -> none  [the longest x1 75.9 us: body(): lax.all_to_all(back_v.astype(jnp.bfloat16), 'ctx', split_axis=0, concat_a...]
    convert_element_type x13 -> x0, other arithmetic: 32.5 us -> none  [the longest x8 18.3 us: attend(): probs = (expo / jnp.sum(expo, axis=-1, keepdims=True)).astype(jnp.bfloat16)]
    all_to_all x3 -> x0, starting transfers between devices: 29.1 us -> none  [the longest x1 10 us: body(): lax.all_to_all(back_v.astype(jnp.bfloat16), 'ctx', split_axis=0, concat_a...]
  transfers between devices with their start and end apart: 4 -> 0, of which waited for: 1 -> 0; matrix products, arithmetic and copies ran while one was open for 3% -> 0% of each run, Pallas kernels for 0% -> 0%
where the time goes in v1:
time: 193 us
  Pallas kernels  180 us (93%)
  local copies, waits for them, and re-layouts  11.7 us (6%)
    pallas_call x1, Pallas kernels, body(): pl.pallas_call(return_kernel, name='back', out_shape=(jax.ShapeDtypeStruc...  72.2 us
    pallas_call x1, Pallas kernels, body(): pl.pallas_call(fetch_kernel, name='fetch', out_shape=(jax.ShapeDtypeStruc...  64 us
    pallas_call x1, Pallas kernels, body(): pl.pallas_call(local_kernel, name='local', out_shape=(jax.ShapeDtypeStruc...  41.3 us
    unnamed x19, local copies, waits for them, and re-layouts  10.6 us

profile of v1, /device:TPU:33, one launch (start us, length us, event | category | flops | bytes accessed | tf_op | source)
XLA Modules:
  0.0 192.9 jit_solution(1160948963704447820)
XLA Ops:
  0.6 0.9 copy.19
  1.6 0.9 copy.16
  2.5 0.2 reshape.34.sel_ref
  2.7 0.0 copy-start.5
  2.7 0.8 copy-done.5
  3.5 0.0 copy-start.6
  3.5 0.8 copy-done.6
  4.4 0.0 copy-start.7
  4.4 0.7 copy-done.7
  5.0 0.0 copy-start.8
  5.1 0.7 copy-done.8
  5.7 64.0 %fetch.1 = (bf16[2,2,16,64,256]{4,3,2,1,0:T(8,128)(2,1)S(1)}, f32[128,8,128]{2,1,0:T(8,128)S(1)}, bf16[32,1280]{1,0:T(8,128)(2,1)S(1)}) custom-call(s32[7680]{0:T(1024)S(1)} %reshape.34.sel_ref, bf16[4,64,128]{2,1,0:T(8,128)(2,1)S(1)} %bitcast.19, bf16[4,64,128]{2,1,0:T(8,128)(2,1)S(1)} %bitcast.20, bf16[4,128]{1,0:T(4,128)(2,1)S(1)} %copy-done.7, ...), custom_call_target="tpu_custom_call" | custom-call | tf_op jit(solution)/shard_map/fetch/pallas_call | solution.py:428
  69.7 0.0 copy-start
  69.7 1.3 copy-done
  71.0 0.0 copy-start.2
  71.0 1.3 copy-done.2
  72.3 0.0 copy-start.3
  72.4 1.2 copy-done.3
  73.6 0.0 copy-start.4
  73.6 1.2 copy-done.4
  74.8 41.3 %local.1 = (bf16[256,2048]{1,0:T(8,128)(2,1)}, bf16[4,1024,256]{2,1,0:T(8,128)(2,1)}, f32[4,64,256]{2,1,0:T(8,128)S(1)}, f32[64,2,8,128]{3,2,1,0:T(8,128)S(1)}, bf16[32,256]{1,0:T(8,128)(2,1)S(1)}) custom-call(bf16[256,2048]{1,0:T(8,128)(2,1)S(1)} %copy-done.3, bf16[256,2048]{1,0:T(8,128)(2,1)S(1)} %copy-done.4, bf16[256,2560]{1,0:T(8,128)(2,1)S(1)} %copy-done.2, ...), custom_call_target="tpu_custom_call" | custom-call | tf_op jit(solution)/shard_map/local/pallas_call | solution.py:448
  116.1 0.0 copy-start.1
  116.1 1.6 copy-done.1
  117.7 72.2 %back.1 = (bf16[30,2,64,256]{3,2,1,0:T(8,128)(2,1)S(1)}, f32[8,128]{1,0:T(8,128)S(1)}, bf16[32,256]{1,0:T(8,128)(2,1)S(1)}) custom-call(bf16[2,2,16,64,256]{4,3,2,1,0:T(8,128)(2,1)S(1)} %bitcast.17, f32[128,8,128]{2,1,0:T(8,128)S(1)} %bitcast.18, bf16[32,256]{1,0:T(8,128)(2,1)S(1)} %get-tuple-element.27.dz_ref), custom_call_target="tpu_custom_call" | custom-call | tf_op jit(solution)/shard_map/back/pallas_call | solution.py:478
  189.8 3.0 %finish.1 = (bf16[256,128]{1,0:T(8,128)(2,1)}, bf16[256,128]{1,0:T(8,128)(2,1)}, bf16[4,128]{1,0:T(4,128)(2,1)}, bf16[4,128]{1,0:T(4,128)(2,1)}, bf16[256,1280]{1,0:T(8,128)(2,1)}) custom-call(s32[7680]{0:T(1024)S(1)} %reshape.34.sel_ref, bf16[30,2,64,256]{3,2,1,0:T(8,128)(2,1)S(1)} %get-tuple-element.28.back_ref, ...), custom_call_target="tpu_custom_call" | custom-call | tf_op jit(solution)/shard_map/finish/pallas_call | solution.py:499
Async XLA Ops:
  2.7 0.8 copy-start.5
  3.5 0.8 copy-start.6
  4.4 0.7 copy-start.7
  5.0 0.7 copy-start.8
  69.7 1.3 copy-start
  71.0 1.3 copy-start.2
  72.3 1.2 copy-start.3
  73.6 1.2 copy-start.4
  116.1 1.6 copy-start.1

commit v2 on v1

v2 whole, which is shorter than its diff:
```python
import functools

import jax
import jax.numpy as jnp
from jax import lax
from jax.experimental import pallas as pl
from jax.experimental.pallas import tpu as pltpu
from jax.sharding import PartitionSpec as P

BLK = 64
PICKS = 15
HD = 128
QB = 4
RANKS = 128
HEADS = 16
LOW = 16
OUTER = RANKS // LOW
HALF = RANKS // 2
SCALE = HD ** -0.5
LOG2E = 1.4426950408889634
BF = jnp.bfloat16
F32 = jnp.float32
MIB = 1 << 20


def reach(parity, j):
    if parity == 0:
        return 1 + (j * (HALF - 1)) // (PICKS - 1)
    return HALF + 1 + (j * (HALF - 2)) // (PICKS - 1)


REACH = [(p, j, reach(p, j)) for p in range(2) for j in range(PICKS)]


def count(conditions):
    return sum(c.astype(jnp.int32) for c in conditions)


def at_ctx(index):
    return {"ctx": index}


def signal(sem, device):
    pl.semaphore_signal(sem, inc=1, device_id=device, device_id_type=pl.DeviceIdType.MESH)


def remote(src, dst, send_sem, recv_sem, device):
    return pltpu.make_async_remote_copy(
        src_ref=src,
        dst_ref=dst,
        send_sem=send_sem,
        recv_sem=recv_sem,
        device_id=device,
        device_id_type=pl.DeviceIdType.MESH,
    )


def nt(a, b):
    return lax.dot_general(a, b, (((1,), (1,)), ((), ())), preferred_element_type=F32)


def nn(a, b):
    return lax.dot_general(a, b, (((1,), (0,)), ((), ())), preferred_element_type=F32)


def scores_backward(k, v, kt, bias, q, do):
    s = nt(k, q) * (SCALE * LOG2E) + bias
    top = jnp.max(s, axis=0, keepdims=True)
    e = jnp.exp2(s - top)
    prob = e * (1.0 / jnp.sum(e, axis=0, keepdims=True))
    dp = nt(v, do)
    delta = jnp.sum(prob * dp, axis=0, keepdims=True)
    ds = (prob * (dp - delta)).astype(BF)
    dv = nn(prob.astype(BF), do)
    dk = nn(ds, q)
    dqt = nn(kt, ds)
    return dqt, dk, dv, delta


def reach_of(parity, j):
    near = 1 + (j * (HALF - 1)) // (PICKS - 1)
    far = HALF + 1 + (j * (HALF - 2)) // (PICKS - 1)
    return jnp.where(parity == 0, near, far)


def each(n, visit):
    def step(i, carry):
        visit(i)
        return carry

    lax.fori_loop(0, n, step, 0)


def attention_kernel(
    sel_ref, k_ref, v_ref, ck_ref, cv_ref, w_ref, q_hbm, do_hbm, x_hbm,
    dq_ref, back_ref, down_ref, csum_ref, dz_ref, dzother_ref, wother_ref,
    q_ref, do_ref, x_ref, out_buf, kv_ref, comp_ref, dkv_ref, dcomp_ref, b_buf, b_sum, a_buf,
    doc, dos, dq_acc, bias_c, bias_s, ck, cv, ckt, kt, dc_acc, dkv_acc, delta_c, delta_s,
    kv_send, kv_recv, g_send, g_recv, a_send, a_recv, b_send, b_recv,
    ra_send, ra_recv, rb_send, rb_recv, w_sems, z_sems, in_sems,
):
    me = lax.axis_index("ctx")
    hd = lax.axis_index("head")
    group = me // LOW
    low = me % LOW
    partner = {"head": 1 - hd}
    tokens = q_ref.shape[0]
    half = w_ref.shape[2]

    x_in = pltpu.make_async_copy(x_hbm, x_ref, in_sems.at[0])
    do_in = pltpu.make_async_copy(do_hbm, do_ref, in_sems.at[1])
    q_in = pltpu.make_async_copy(q_hbm, q_ref, in_sems.at[2])
    x_in.start()
    do_in.start()
    q_in.start()

    barrier = pltpu.get_barrier_semaphore()

    @functools.partial(each, LOW)
    def _(a):
        @pl.when(a != low)
        def _():
            signal(barrier, at_ctx(group * LOW + a))

    @functools.partial(each, OUTER)
    def _(g):
        @pl.when(g != group)
        def _():
            signal(barrier, at_ctx(g * LOW + low))

    @functools.partial(each, 2 * PICKS)
    def _(n):
        r = reach_of(n // PICKS, n % PICKS)

        @pl.when(me >= r)
        def _():
            signal(barrier, at_ctx(me - r))

        @pl.when(me + r < RANKS)
        def _():
            signal(barrier, at_ctx(me + r))

    signal(barrier, partner)

    comp_ref[pl.ds(me, 1), 0:4, :] = ck_ref[...].astype(F32)[None]
    comp_ref[pl.ds(me, 1), 4:8, :] = cv_ref[...].astype(F32)[None]

    @functools.partial(each, OUTER)
    def _(g):
        @pl.when(g > group)
        def _():
            comp_ref[pl.ds(g * LOW, LOW)] = jnp.zeros((LOW, 8, HD), F32)

    for b in range(QB):
        @functools.partial(each, PICKS)
        def _(j):
            r = reach_of(b % 2, j)
            asker = jnp.minimum(me + r, RANKS - 1)
            local = sel_ref[(asker * QB + b) * PICKS + j] & (QB - 1)
            out_buf[b, j, :, 0:HD] = k_ref[local]
            out_buf[b, j, :, HD:] = v_ref[local]

            @pl.when(me < r)
            def _():
                kv_ref[b, j] = jnp.zeros((BLK, 2 * HD), BF)

        kv_ref[b, PICKS, :, 0:HD] = k_ref[b]
        kv_ref[b, PICKS, :, HD:] = v_ref[b]

    peers = count(
        [me + r < RANKS for _, _, r in REACH] + [me >= r for _, _, r in REACH]
    )
    pl.semaphore_wait(barrier, peers + (LOW - 1) + (OUTER - 1) + 1)

    def a_copy(a, slot):
        return remote(
            comp_ref.at[slot], comp_ref.at[slot], a_send.at[a], a_recv.at[slot % LOW],
            at_ctx(group * LOW + a),
        )

    def b_copy(g, source):
        rows = pl.ds(source * LOW, LOW)
        return remote(
            comp_ref.at[rows], comp_ref.at[rows], b_send.at[g], b_recv.at[source],
            at_ctx(g * LOW + low),
        )

    def kv_copy(b, j, target):
        return remote(
            out_buf.at[b, j], kv_ref.at[b, j], kv_send.at[b, j], kv_recv.at[b, j], at_ctx(target)
        )

    def grad_copy(b, j, target):
        return remote(
            dkv_ref.at[b, j], back_ref.at[b, j], g_send.at[b, j], g_recv.at[b, j], at_ctx(target)
        )

    def rb_copy(g, source):
        return remote(
            dcomp_ref.at[pl.ds(g * LOW, LOW)], b_buf.at[source], rb_send.at[g], rb_recv.at[source],
            at_ctx(g * LOW + low),
        )

    def ra_copy(a, source):
        return remote(
            b_sum.at[a], a_buf.at[source], ra_send.at[a], ra_recv.at[source],
            at_ctx(group * LOW + a),
        )

    w_copy = remote(w_ref.at[1 - hd], wother_ref, w_sems.at[0], w_sems.at[1], partner)
    z_copy = remote(dz_ref, dzother_ref, z_sems.at[0], z_sems.at[1], partner)

    def others_low(visit):
        @functools.partial(each, LOW)
        def _(a):
            @pl.when(a != low)
            def _():
                visit(a)

    def outer_where(test, visit):
        @functools.partial(each, OUTER)
        def _(g):
            @pl.when(test(g))
            def _():
                visit(g)

    def askers(b, visit):
        @functools.partial(each, PICKS)
        def _(j):
            r = reach_of(b % 2, j)

            @pl.when(me + r < RANKS)
            def _():
                visit(j, me + r)

    def owners(b, visit):
        @functools.partial(each, PICKS)
        def _(j):
            r = reach_of(b % 2, j)

            @pl.when(me >= r)
            def _():
                visit(j, me - r)

    others_low(lambda a: a_copy(a, me).start())
    askers(0, lambda j, t: kv_copy(0, j, t).start())
    others_low(lambda a: a_copy(a, group * LOW + a).wait_recv())
    outer_where(lambda g: g > group, lambda g: b_copy(g, group).start())
    for b in range(1, QB):
        askers(b, lambda j, t: kv_copy(b, j, t).start())
    w_copy.start()

    row = lax.broadcasted_iota(jnp.int32, (RANKS * QB, tokens), 0)
    col = lax.broadcasted_iota(jnp.int32, (RANKS * QB, tokens), 1)
    bias_c[...] = jnp.where(row <= me * QB + col // BLK, 0.0, -jnp.inf)
    srow = lax.broadcasted_iota(jnp.int32, (BLK, 4 * BLK), 0)
    scol = lax.broadcasted_iota(jnp.int32, (BLK, 4 * BLK), 1) % BLK
    own_bias = jnp.where(srow <= scol, 0.0, -jnp.inf)
    for p, j, r in REACH:
        bias_s[p, j * BLK:(j + 1) * BLK, :] = jnp.full(
            (BLK, 4 * BLK), jnp.where(me >= r, 0.0, -jnp.inf), F32
        )
    for p in range(2):
        bias_s[p, PICKS * BLK:, :] = own_bias
    x_in.wait()
    do_in.wait()
    gate = jax.nn.sigmoid(nt(x_ref[:, 0:half], w_ref[0]) + nt(x_ref[:, half:], w_ref[1]))
    for h in range(HEADS):
        slab = do_ref[:, h * HD:(h + 1) * HD].astype(F32)
        doc[:, h * HD:(h + 1) * HD] = (gate[:, h:h + 1] * slab).astype(BF)
        dos[:, h * HD:(h + 1) * HD] = (gate[:, HEADS + h:HEADS + h + 1] * slab).astype(BF)
    q_in.wait()

    outer_where(lambda g: g < group, lambda g: b_copy(g, g).wait_recv())
    pairs = comp_ref[...].reshape(RANKS // 2, 2, 8, HD)
    even, odd = pairs[:, 0], pairs[:, 1]
    top_rows = lax.broadcasted_iota(jnp.int32, (RANKS // 2, 8, HD), 1) < 4
    swap = lambda z: pltpu.roll(z, 4, 1)
    keys_c = jnp.where(top_rows, even, swap(odd)).reshape(RANKS * 4, HD)
    vals_c = jnp.where(top_rows, swap(even), odd).reshape(RANKS * 4, HD)
    ck[...] = keys_c.astype(BF)
    cv[...] = vals_c.astype(BF)
    ckt[...] = keys_c.T.astype(BF)
    dc_acc[...] = jnp.zeros_like(dc_acc)

    @functools.partial(each, HEADS)
    def _(h):
        lanes = pl.ds(pl.multiple_of(h * HD, HD), HD)
        dqt, dk, dv, delta = scores_backward(
            ck[...], cv[...], ckt[...], bias_c[...], q_ref[:, lanes], doc[:, lanes]
        )
        dq_acc[:, lanes] = dqt.T
        dc_acc[0] += dk
        dc_acc[1] += dv
        delta_c[pl.ds(h, 1), :] = delta

    dck = (dc_acc[0] * SCALE).reshape(RANKS // 2, 8, HD)
    dcv = dc_acc[1].reshape(RANKS // 2, 8, HD)
    dcomp_ref[...] = jnp.stack(
        [jnp.where(top_rows, dck, swap(dcv)), jnp.where(top_rows, swap(dck), dcv)], axis=1
    ).reshape(RANKS, 8, HD)
    outer_where(lambda g: g < group, lambda g: rb_copy(g, group).start())

    @functools.partial(each, QB)
    def _(b):
        owners(b, lambda j, t: kv_copy(b, j, t).wait_recv())
        rows = pl.ds(pl.multiple_of(b * BLK, BLK), BLK)
        keys_all = (PICKS + 1) * BLK
        kt[...] = kv_ref[b, :, :, 0:HD].reshape(keys_all, HD).astype(F32).T.astype(BF)
        dkv_acc[...] = jnp.zeros_like(dkv_acc)
        bias = bias_s.at[b % 2]

        @functools.partial(each, 4)
        def _(g):
            lanes = [pl.ds(pl.multiple_of((g + 4 * i) * HD, HD), HD) for i in range(4)]
            q = jnp.concatenate([q_ref[rows, l] for l in lanes], axis=0)
            do = jnp.concatenate([dos[rows, l] for l in lanes], axis=0)
            dqt, dk, dv, delta = scores_backward(
                kv_ref[b, :, :, 0:HD].reshape(keys_all, HD),
                kv_ref[b, :, :, HD:].reshape(keys_all, HD),
                kt[...], bias[...], q, do,
            )
            dq = dqt.T
            for i in range(4):
                total = (dq[i * BLK:(i + 1) * BLK] + dq_acc[rows, lanes[i]]) * SCALE
                dq_ref[rows, lanes[i]] = total.astype(BF)
            dkv_acc[:, 0:HD] += dk
            dkv_acc[:, HD:] += dv
            delta_s[b, pl.ds(g, 1), :] = delta

        factor = jnp.where(
            lax.broadcasted_iota(jnp.int32, (1, 2 * HD), 1) < HD, jnp.float32(SCALE), 1.0
        )
        total = dkv_acc[...] * factor
        dkv_ref[b] = total[0:PICKS * BLK].astype(BF).reshape(PICKS, BLK, 2 * HD)
        down_ref[b] = total[PICKS * BLK:]
        owners(b, lambda j, t: grad_copy(b, j, t).start())

    gate_t = jax.nn.sigmoid(nt(w_ref[0], x_ref[:, 0:half]) + nt(w_ref[1], x_ref[:, half:]))
    dz_ref[0:HEADS, :] = (delta_c[...] * (1.0 - gate_t[0:HEADS])).astype(BF)
    columns = []
    for b in range(QB):
        columns.append(
            jnp.concatenate([delta_s[b, :, i * BLK:(i + 1) * BLK] for i in range(4)], axis=0)
        )
    sel = jnp.concatenate(columns, axis=1)
    dz_ref[HEADS:, :] = (sel * (1.0 - gate_t[HEADS:])).astype(BF)
    z_copy.start()

    b_sum[...] = dcomp_ref[pl.ds(group * LOW, LOW)]

    def add_outer(g):
        rb_copy(g, g).wait_recv()
        b_sum[...] += b_buf[g]

    outer_where(lambda g: g > group, add_outer)
    others_low(lambda a: ra_copy(a, low).start())
    a_buf[pl.ds(low, 1)] = b_sum[pl.ds(low, 1)]
    others_low(lambda a: ra_copy(a, a).wait_recv())
    csum_ref[...] = jnp.sum(a_buf[...], axis=0)

    w_copy.wait_recv()
    z_copy.wait_recv()
    for b in range(QB):
        askers(b, lambda j, t: grad_copy(b, j, t).wait_recv())
    for b in range(QB):
        askers(b, lambda j, t: kv_copy(b, j, t).wait_send())
        owners(b, lambda j, t: grad_copy(b, j, t).wait_send())
    others_low(lambda a: a_copy(a, me).wait_send())
    outer_where(lambda g: g > group, lambda g: b_copy(g, group).wait_send())
    outer_where(lambda g: g < group, lambda g: rb_copy(g, group).wait_send())
    others_low(lambda a: ra_copy(a, low).wait_send())
    w_copy.wait_send()
    z_copy.wait_send()


def finish_kernel(
    sel_ref, back_ref, down_ref, csum_ref, dz_ref, dzother_ref, w_ref, wother_ref,
    dk_ref, dv_ref, dck_ref, dcv_ref, dx_ref, acc,
):
    me = lax.axis_index("ctx")
    hd = lax.axis_index("head")
    acc[...] = down_ref[...]
    for p, j, r in REACH:
        @pl.when(me + r < RANKS)
        def _():
            for i in range(2):
                local = sel_ref[((me + r) * QB + p + 2 * i) * PICKS + j] & (QB - 1)
                acc[local] += back_ref[p + 2 * i, j].astype(F32)
    for b in range(QB):
        dk_ref[b * BLK:(b + 1) * BLK, :] = acc[b, :, 0:HD].astype(BF)
        dv_ref[b * BLK:(b + 1) * BLK, :] = acc[b, :, HD:].astype(BF)
    dck_ref[...] = csum_ref[0:4, :].astype(BF)
    dcv_ref[...] = csum_ref[4:8, :].astype(BF)
    mine = lax.dot_general(
        dz_ref[...], w_ref[hd], (((0,), (0,)), ((), ())), preferred_element_type=F32
    )
    other = lax.dot_general(
        dzother_ref[...], wother_ref[...], (((0,), (0,)), ((), ())), preferred_element_type=F32
    )
    dx_ref[...] = (mine + other).astype(BF)


VM = pl.BlockSpec(memory_space=pltpu.VMEM)
SM = pl.BlockSpec(memory_space=pltpu.SMEM)


def body(queries, keys, values, comp_keys, comp_values, selected, inputs, w_gate, d_out):
    tokens = queries.shape[0]
    width = inputs.shape[1]
    half = width // 2
    dma = lambda *n: pltpu.SemaphoreType.DMA(n)
    vm = lambda *shape: pltpu.VMEM(shape, BF)
    vf = lambda *shape: pltpu.VMEM(shape, F32)
    sel = selected.reshape(-1)
    w2 = w_gate.T.reshape(2 * HEADS, 2, half).transpose(1, 0, 2)
    keys_all = (PICKS + 1) * BLK
    blocks = (QB, BLK, HD)

    dq, back, down, csum, dz, dz_other, w_other = pl.pallas_call(
        attention_kernel,
        name="attention",
        out_shape=(
            jax.ShapeDtypeStruct(queries.shape, BF),
            jax.ShapeDtypeStruct((QB, PICKS, BLK, 2 * HD), BF),
            jax.ShapeDtypeStruct((QB, BLK, 2 * HD), F32),
            jax.ShapeDtypeStruct((8, HD), F32),
            jax.ShapeDtypeStruct((2 * HEADS, tokens), BF),
            jax.ShapeDtypeStruct((2 * HEADS, tokens), BF),
            jax.ShapeDtypeStruct((2 * HEADS, half), BF),
        ),
        in_specs=[SM] + [VM] * 5 + [pl.BlockSpec(memory_space=pl.ANY)] * 3,
        out_specs=(VM,) * 7,
        scratch_shapes=[
            vm(*queries.shape), vm(*d_out.shape), vm(*inputs.shape),
            vm(QB, PICKS, BLK, 2 * HD), vm(QB, PICKS + 1, BLK, 2 * HD), vf(RANKS, 8, HD),
            vm(QB, PICKS, BLK, 2 * HD), vf(RANKS, 8, HD),
            vf(OUTER, LOW, 8, HD), vf(LOW, 8, HD), vf(LOW, 8, HD),
            vm(*queries.shape), vm(*queries.shape), vf(*queries.shape),
            vf(RANKS * QB, tokens), vf(2, keys_all, 4 * BLK),
            vm(RANKS * QB, HD), vm(RANKS * QB, HD), vm(HD, RANKS * QB), vm(HD, keys_all),
            vf(2, RANKS * QB, HD), vf(keys_all, 2 * HD), vf(HEADS, tokens), vf(QB, 4, 4 * BLK),
            dma(QB, PICKS), dma(QB, PICKS), dma(QB, PICKS), dma(QB, PICKS),
            dma(LOW), dma(LOW), dma(OUTER), dma(OUTER),
            dma(LOW), dma(LOW), dma(OUTER), dma(OUTER), dma(2), dma(2), dma(3),
        ],
        compiler_params=pltpu.CompilerParams(
            collective_id=0, has_side_effects=True, vmem_limit_bytes=48 * MIB
        ),
    )(
        sel, keys.reshape(blocks), values.reshape(blocks), comp_keys, comp_values, w2,
        queries, d_out, inputs,
    )

    dk, dv, dck, dcv, dx = pl.pallas_call(
        finish_kernel,
        name="finish",
        out_shape=(
            jax.ShapeDtypeStruct((tokens, HD), BF),
            jax.ShapeDtypeStruct((tokens, HD), BF),
            jax.ShapeDtypeStruct((QB, HD), BF),
            jax.ShapeDtypeStruct((QB, HD), BF),
            jax.ShapeDtypeStruct((tokens, half), BF),
        ),
        in_specs=[SM] + [VM] * 7,
        out_specs=(VM,) * 5,
        scratch_shapes=[pltpu.VMEM((QB, BLK, 2 * HD), F32)],
        compiler_params=pltpu.CompilerParams(vmem_limit_bytes=24 * MIB),
    )(sel, back, down, csum, dz, dz_other, w2, w_other)
    return dq, dk, dv, dck, dcv, dx


def solution(mesh):
    split = P("ctx", "head")
    in_specs = (split, split, split, split, split, P(), P("ctx", None), P(None, "head"), split)
    return jax.shard_map(body, mesh=mesh, in_specs=in_specs, out_specs=(split,) * 6, check_vma=False)
```

time: 193 us -> 135 us (0.70)
  Pallas kernels: 180 us -> 122 us
    pallas_call x3 -> x1, Pallas kernels: 177 us -> 119 us  [body(): pl.pallas_call(attention_kernel, name='attention', out_shape=(jax.ShapeDt...]
    unnamed x19 -> x18, local copies, waits for them, and re-layouts: 10.6 us -> 10.2 us
where the time goes in v2:
time: 135 us; the launch traced here: 134 us
  Pallas kernels  122 us (90%)
  local copies, waits for them, and re-layouts  11.3 us (8%)
    pallas_call x1, Pallas kernels, body(): pl.pallas_call(attention_kernel, name='attention', out_shape=(jax.ShapeDt...  119 us
    unnamed x18, local copies, waits for them, and re-layouts  10.2 us
    pallas_call x1, Pallas kernels, body(): pl.pallas_call(finish_kernel, name='finish', out_shape=(jax.ShapeDtypeStr...  3.03 us

profile of v2, /device:TPU:33, one launch (start us, length us, event | category | flops | bytes accessed | tf_op | source)
XLA Modules:
  0.0 133.9 jit_solution(17409680181397315331)
XLA Ops:
  0.6 0.9 copy.15
  1.5 0.2 reshape.24.sel_ref
  1.8 0.9 copy.19
  2.7 0.0 copy-start.1
  2.7 1.3 copy-done.1
  4.0 0.0 copy-start.2
  4.0 1.2 copy-done.2
  5.2 0.0 copy-start.3
  5.2 1.2 copy-done.3
  6.5 0.0 copy-start.4
  6.5 0.8 copy-done.4
  7.3 0.0 copy-start.5
  7.3 0.8 copy-done.5
  8.1 0.0 copy-start.6
  8.1 0.7 copy-done.6
  8.8 0.0 copy-start.7
  8.8 0.7 copy-done.7
  9.5 118.9 %attention.1 = (bf16[256,2048]{1,0:T(8,128)(2,1)S(1)}, bf16[4,15,64,256]{3,2,1,0:T(8,128)(2,1)}, f32[4,64,256]{2,1,0:T(8,128)S(1)}, f32[8,128]{1,0:T(8,128)S(1)}...) custom-call(s32[7680]{0:T(1024)S(1)} %reshape.24.sel_ref, ...), custom_call_target="tpu_custom_call" | custom-call | tf_op jit(solution)/shard_map/attention/pallas_call | solution.py:420
  128.4 0.0 copy-start
  128.4 1.5 %copy-done = bf16[4,15,64,256]{3,2,1,0:T(8,128)(2,1)S(1)} copy-done((bf16[4,15,64,256]{3,2,1,0:T(8,128)(2,1)S(1)}, bf16[4,15,64,256]{3,2,1,0:T(8,128)(2,1)}, u32[]{:S(2)}) %copy-start) | copy-done | bytes 1966104
  129.9 3.0 %finish.1 = (bf16[256,128]{1,0:T(8,128)(2,1)}, bf16[256,128]{1,0:T(8,128)(2,1)}, bf16[4,128]{1,0:T(4,128)(2,1)}, bf16[4,128]{1,0:T(4,128)(2,1)}, bf16[256,1280]{1,0:T(8,128)(2,1)}) custom-call(s32[7680]{0:T(1024)S(1)} %reshape.24.sel_ref, bf16[4,15,64,256]{3,2,1,0:T(8,128)(2,1)S(1)} %copy-done, f32[4,64,256]{2,1,0:T(8,128)S(1)} %get-tuple-element.20.down_ref, ...), custom_call_target="tpu_custom_call" | custom-call | tf_op jit(solution)/shard_map/finish/pallas_call | solution.py:455
  133.0 1.0 copy.21
Async XLA Ops:
  2.7 1.3 copy-start.1
  4.0 1.2 copy-start.2
  5.2 1.2 copy-start.3
  6.5 0.8 copy-start.4
  7.3 0.8 copy-start.5
  8.1 0.7 copy-start.6
  8.8 0.7 copy-start.7
  128.4 1.5 %copy-start = (bf16[4,15,64,256]{3,2,1,0:T(8,128)(2,1)S(1)}, bf16[4,15,64,256]{3,2,1,0:T(8,128)(2,1)}, u32[]{:S(2)}) copy-start(bf16[4,15,64,256]{3,2,1,0:T(8,128)(2,1)} %get-tuple-element.19.back_ref) | copy-start | bytes 5898244

commit v3 on v2

--- a/solution.py
+++ b/solution.py
@@ -16,6 +16,8 @@
 LOW = 16
 OUTER = RANKS // LOW
 HALF = RANKS // 2
+PLANE = 32
+RELAYS = PICKS // 2
 SCALE = HD ** -0.5
 LOG2E = 1.4426950408889634
 BF = jnp.bfloat16
@@ -83,6 +85,16 @@
     return jnp.where(parity == 0, near, far)
 
 
+def relayed(j, source, target):
+    odd = (j % 2 == 1) & (source // PLANE != target // PLANE)
+    return odd & (source % PLANE != target % PLANE)
+
+
+def stop(j, source, target):
+    relay = target // PLANE * PLANE + source % PLANE
+    return jnp.where(relayed(j, source, target), relay, target)
+
+
 def each(n, visit):
     def step(i, carry):
         visit(i)
@@ -92,11 +104,11 @@
 
 
 def attention_kernel(
-    sel_ref, k_ref, v_ref, ck_ref, cv_ref, w_ref, q_hbm, do_hbm, x_hbm,
-    dq_ref, back_ref, down_ref, csum_ref, dz_ref, dzother_ref, wother_ref,
-    q_ref, do_ref, x_ref, out_buf, kv_ref, comp_ref, dkv_ref, dcomp_ref, b_buf, b_sum, a_buf,
+    sel_ref, ck_ref, cv_ref, k_hbm, v_hbm, w_hbm, q_hbm, do_hbm, x_hbm,
+    dq_ref, down_ref, csum_ref, dz_ref, dzother_ref, wother_ref,
+    k_ref, v_ref, w_ref, q_ref, do_ref, x_ref, back_ref, relay_f, relay_b, out_buf, kv_ref, comp_ref, dkv_ref, dcomp_ref, b_buf, b_sum, a_buf,
     doc, dos, dq_acc, bias_c, bias_s, ck, cv, ckt, kt, dc_acc, dkv_acc, delta_c, delta_s,
-    kv_send, kv_recv, g_send, g_recv, a_send, a_recv, b_send, b_recv,
+    kv_send, kv_recv, g_send, g_recv, f_send, f_recv, h_send, h_recv, a_send, a_recv, b_send, b_recv,
     ra_send, ra_recv, rb_send, rb_recv, w_sems, z_sems, in_sems,
 ):
     me = lax.axis_index("ctx")
@@ -105,8 +117,15 @@
     low = me % LOW
     partner = {"head": 1 - hd}
     tokens = q_ref.shape[0]
-    half = w_ref.shape[2]
-
+    half = w_ref.shape[1] // 2
+    place = me % PLANE
+
+    k_in = pltpu.make_async_copy(k_hbm, k_ref, in_sems.at[3])
+    v_in = pltpu.make_async_copy(v_hbm, v_ref, in_sems.at[4])
+    w_in = pltpu.make_async_copy(w_hbm, w_ref, in_sems.at[5])
+    k_in.start()
+    v_in.start()
+    w_in.start()
     x_in = pltpu.make_async_copy(x_hbm, x_ref, in_sems.at[0])
     do_in = pltpu.make_async_copy(do_hbm, do_ref, in_sems.at[1])
     q_in = pltpu.make_async_copy(q_hbm, q_ref, in_sems.at[2])
@@ -116,11 +135,11 @@
 
     barrier = pltpu.get_barrier_semaphore()
 
-    @functools.partial(each, LOW)
+    @functools.partial(each, PLANE)
     def _(a):
-        @pl.when(a != low)
-        def _():
-            signal(barrier, at_ctx(group * LOW + a))
+        @pl.when(a != place)
+        def _():
+            signal(barrier, at_ctx(me - place + a))
 
     @functools.partial(each, OUTER)
     def _(g):
@@ -151,12 +170,14 @@
         def _():
             comp_ref[pl.ds(g * LOW, LOW)] = jnp.zeros((LOW, 8, HD), F32)
 
+    k_in.wait()
+    v_in.wait()
     for b in range(QB):
         @functools.partial(each, PICKS)
         def _(j):
             r = reach_of(b % 2, j)
             asker = jnp.minimum(me + r, RANKS - 1)
-            local = sel_ref[(asker * QB + b) * PICKS + j] & (QB - 1)
+            local = sel_ref[j, asker * QB + b] & (QB - 1)
             out_buf[b, j, :, 0:HD] = k_ref[local]
             out_buf[b, j, :, HD:] = v_ref[local]
 
@@ -170,7 +191,7 @@
     peers = count(
         [me + r < RANKS for _, _, r in REACH] + [me >= r for _, _, r in REACH]
     )
-    pl.semaphore_wait(barrier, peers + (LOW - 1) + (OUTER - 1) + 1)
+    pl.semaphore_wait(barrier, peers + (PLANE - 1) + (OUTER - 1) + 1)
 
     def a_copy(a, slot):
         return remote(
@@ -185,6 +206,30 @@
             at_ctx(g * LOW + low),
         )
 
+    def relay_copy(b, j, target):
+        return remote(
+            out_buf.at[b, j], relay_f.at[b, j // 2], kv_send.at[b, j], f_recv.at[b, j // 2],
+            at_ctx(target),
+        )
+
+    def forward_copy(b, i, target):
+        return remote(
+            relay_f.at[b, i], kv_ref.at[b, 2 * i + 1], f_send.at[b, i],
+            kv_recv.at[b, 2 * i + 1], at_ctx(target),
+        )
+
+    def grad_relay_copy(b, j, target):
+        return remote(
+            dkv_ref.at[b, j], relay_b.at[b, j // 2], g_send.at[b, j], h_recv.at[b, j // 2],
+            at_ctx(target),
+        )
+
+    def grad_forward_copy(b, i, target):
+        return remote(
+            relay_b.at[b, i], back_ref.at[b, 2 * i + 1], h_send.at[b, i],
+            g_recv.at[b, 2 * i + 1], at_ctx(target),
+        )
+
     def kv_copy(b, j, target):
         return remote(
             out_buf.at[b, j], kv_ref.at[b, j], kv_send.at[b, j], kv_recv.at[b, j], at_ctx(target)
@@ -207,7 +252,8 @@
             at_ctx(group * LOW + a),
         )
 
-    w_copy = remote(w_ref.at[1 - hd], wother_ref, w_sems.at[0], w_sems.at[1], partner)
+    theirs = pl.ds(pl.multiple_of((1 - hd) * half, HD), half)
+    w_copy = remote(w_ref.at[:, theirs], wother_ref, w_sems.at[0], w_sems.at[1], partner)
     z_copy = remote(dz_ref, dzother_ref, z_sems.at[0], z_sems.at[1], partner)
 
     def others_low(visit):
@@ -242,12 +288,50 @@
             def _():
                 visit(j, me - r)
 
+    def fetch_forwards(b, i, visit):
+        r = reach_of(b % 2, 2 * i + 1)
+        planes = (place + r) // PLANE
+        source = me - PLANE * planes
+        target = source + r
+
+        @pl.when((planes > 0) & (source >= 0) & (target != me))
+        def _():
+            visit(target)
+
+    def grad_forwards(b, i, visit):
+        r = reach_of(b % 2, 2 * i + 1)
+        planes = (r - place + PLANE - 1) // PLANE
+        source = me + PLANE * planes
+        target = source - r
+
+        @pl.when((r > place) & (source < RANKS) & (target != me))
+        def _():
+            visit(target)
+
+    def send_relayed(b):
+        def visit(j, t):
+            @pl.when(relayed(j, me, t))
+            def _():
+                relay_copy(b, j, stop(j, me, t)).start()
+
+        askers(b, visit)
+
+    def send_direct(b):
+        def visit(j, t):
+            @pl.when(jnp.logical_not(relayed(j, me, t)))
+            def _():
+                kv_copy(b, j, t).start()
+
+        askers(b, visit)
+
     others_low(lambda a: a_copy(a, me).start())
-    askers(0, lambda j, t: kv_copy(0, j, t).start())
+    for b in range(QB):
+        send_relayed(b)
     others_low(lambda a: a_copy(a, group * LOW + a).wait_recv())
     outer_where(lambda g: g > group, lambda g: b_copy(g, group).start())
-    for b in range(1, QB):
-        askers(b, lambda j, t: kv_copy(b, j, t).start())
+    for b in range(QB):
+        send_direct(b)
+    w_in.wait()
     w_copy.start()
 
     row = lax.broadcasted_iota(jnp.int32, (RANKS * QB, tokens), 0)
@@ -264,7 +348,7 @@
         bias_s[p, PICKS * BLK:, :] = own_bias
     x_in.wait()
     do_in.wait()
-    gate = jax.nn.sigmoid(nt(x_ref[:, 0:half], w_ref[0]) + nt(x_ref[:, half:], w_ref[1]))
+    gate = jax.nn.sigmoid(nt(x_ref[...], w_ref[...]))
     for h in range(HEADS):
         slab = do_ref[:, h * HD:(h + 1) * HD].astype(F32)
         doc[:, h * HD:(h + 1) * HD] = (gate[:, h:h + 1] * slab).astype(BF)
@@ -285,6 +369,18 @@
 
     @functools.partial(each, HEADS)
     def _(h):
+        @pl.when(h < QB * RELAYS // 2)
+        def _():
+            for i in range(2):
+                n = 2 * h + i
+                b, entry = n // RELAYS, n % RELAYS
+
+                def pass_on(target):
+                    relay_copy(b, 2 * entry + 1, target).wait_recv()
+                    forward_copy(b, entry, target).start()
+
+                fetch_forwards(b, entry, pass_on)
+
         lanes = pl.ds(pl.multiple_of(h * HD, HD), HD)
         dqt, dk, dv, delta = scores_backward(
             ck[...], cv[...], ckt[...], bias_c[...], q_ref[:, lanes], doc[:, lanes]
@@ -334,9 +430,31 @@
         total = dkv_acc[...] * factor
         dkv_ref[b] = total[0:PICKS * BLK].astype(BF).reshape(PICKS, BLK, 2 * HD)
         down_ref[b] = total[PICKS * BLK:]
-        owners(b, lambda j, t: grad_copy(b, j, t).start())
-
-    gate_t = jax.nn.sigmoid(nt(w_ref[0], x_ref[:, 0:half]) + nt(w_ref[1], x_ref[:, half:]))
+
+        def send_grad(j, t):
+            hop = relayed(j, me, t) & (b < QB - 1)
+
+            @pl.when(hop)
+            def _():
+                grad_relay_copy(b, j, stop(j, me, t)).start()
+
+            @pl.when(jnp.logical_not(hop))
+            def _():
+                grad_copy(b, j, t).start()
+
+        owners(b, send_grad)
+
+        @pl.when(b > 0)
+        def _():
+            @functools.partial(each, RELAYS)
+            def _(i):
+                def pass_on(target):
+                    grad_relay_copy(b - 1, 2 * i + 1, target).wait_recv()
+                    grad_forward_copy(b - 1, i, target).start()
+
+                grad_forwards(b - 1, i, pass_on)
+
+    gate_t = jax.nn.sigmoid(nt(w_ref[...], x_ref[...]))
     dz_ref[0:HEADS, :] = (delta_c[...] * (1.0 - gate_t[0:HEADS])).astype(BF)
     columns = []
     for b in range(QB):
@@ -356,16 +474,33 @@
     outer_where(lambda g: g > group, add_outer)
     others_low(lambda a: ra_copy(a, low).start())
     a_buf[pl.ds(low, 1)] = b_sum[pl.ds(low, 1)]
+
+    def add_arrived(b):
+        def visit(j, t):
+            grad_copy(b, j, t).wait_recv()
+            local = sel_ref[j, t * QB + b] & (QB - 1)
+            term = back_ref[b, j].astype(F32)
+            for c in range(QB):
+                down_ref[c] += jnp.where(local == c, term, 0.0)
+
+        askers(b, visit)
+
+    for b in range(QB):
+        add_arrived(b)
     others_low(lambda a: ra_copy(a, a).wait_recv())
     csum_ref[...] = jnp.sum(a_buf[...], axis=0)
-
     w_copy.wait_recv()
     z_copy.wait_recv()
     for b in range(QB):
-        askers(b, lambda j, t: grad_copy(b, j, t).wait_recv())
-    for b in range(QB):
         askers(b, lambda j, t: kv_copy(b, j, t).wait_send())
         owners(b, lambda j, t: grad_copy(b, j, t).wait_send())
+
+        @functools.partial(each, RELAYS)
+        def _(i):
+            fetch_forwards(b, i, lambda t: forward_copy(b, i, t).wait_send())
+            if b < QB - 1:
+                grad_forwards(b, i, lambda t: grad_forward_copy(b, i, t).wait_send())
+
     others_low(lambda a: a_copy(a, me).wait_send())
     outer_where(lambda g: g > group, lambda g: b_copy(g, group).wait_send())
     outer_where(lambda g: g < group, lambda g: rb_copy(g, group).wait_send())
@@ -375,30 +510,18 @@
 
 
 def finish_kernel(
-    sel_ref, back_ref, down_ref, csum_ref, dz_ref, dzother_ref, w_ref, wother_ref,
-    dk_ref, dv_ref, dck_ref, dcv_ref, dx_ref, acc,
+    down_ref, csum_ref, dz_ref, dzother_ref, w_ref, wother_ref, dk_ref, dv_ref, dck_ref, dcv_ref, dx_ref
 ):
-    me = lax.axis_index("ctx")
     hd = lax.axis_index("head")
-    acc[...] = down_ref[...]
-    for p, j, r in REACH:
-        @pl.when(me + r < RANKS)
-        def _():
-            for i in range(2):
-                local = sel_ref[((me + r) * QB + p + 2 * i) * PICKS + j] & (QB - 1)
-                acc[local] += back_ref[p + 2 * i, j].astype(F32)
+    half = wother_ref.shape[1]
+    mine = pl.ds(pl.multiple_of(hd * half, HD), half)
     for b in range(QB):
-        dk_ref[b * BLK:(b + 1) * BLK, :] = acc[b, :, 0:HD].astype(BF)
-        dv_ref[b * BLK:(b + 1) * BLK, :] = acc[b, :, HD:].astype(BF)
+        dk_ref[b * BLK:(b + 1) * BLK, :] = down_ref[b, :, 0:HD].astype(BF)
+        dv_ref[b * BLK:(b + 1) * BLK, :] = down_ref[b, :, HD:].astype(BF)
     dck_ref[...] = csum_ref[0:4, :].astype(BF)
     dcv_ref[...] = csum_ref[4:8, :].astype(BF)
-    mine = lax.dot_general(
-        dz_ref[...], w_ref[hd], (((0,), (0,)), ((), ())), preferred_element_type=F32
-    )
-    other = lax.dot_general(
-        dzother_ref[...], wother_ref[...], (((0,), (0,)), ((), ())), preferred_element_type=F32
-    )
-    dx_ref[...] = (mine + other).astype(BF)
+    tn = lambda a, c: lax.dot_general(a, c, (((0,), (0,)), ((), ())), preferred_element_type=F32)
+    dx_ref[...] = (tn(dz_ref[...], w_ref[:, mine]) + tn(dzother_ref[...], wother_ref[...])).astype(BF)
 
 
 VM = pl.BlockSpec(memory_space=pltpu.VMEM)
@@ -412,27 +535,28 @@
     dma = lambda *n: pltpu.SemaphoreType.DMA(n)
     vm = lambda *shape: pltpu.VMEM(shape, BF)
     vf = lambda *shape: pltpu.VMEM(shape, F32)
-    sel = selected.reshape(-1)
-    w2 = w_gate.T.reshape(2 * HEADS, 2, half).transpose(1, 0, 2)
+    sel = selected.T
+    wt = w_gate.T
     keys_all = (PICKS + 1) * BLK
     blocks = (QB, BLK, HD)
 
-    dq, back, down, csum, dz, dz_other, w_other = pl.pallas_call(
+    dq, down, csum, dz, dz_other, w_other = pl.pallas_call(
         attention_kernel,
         name="attention",
         out_shape=(
             jax.ShapeDtypeStruct(queries.shape, BF),
-            jax.ShapeDtypeStruct((QB, PICKS, BLK, 2 * HD), BF),
             jax.ShapeDtypeStruct((QB, BLK, 2 * HD), F32),
             jax.ShapeDtypeStruct((8, HD), F32),
             jax.ShapeDtypeStruct((2 * HEADS, tokens), BF),
             jax.ShapeDtypeStruct((2 * HEADS, tokens), BF),
             jax.ShapeDtypeStruct((2 * HEADS, half), BF),
         ),
-        in_specs=[SM] + [VM] * 5 + [pl.BlockSpec(memory_space=pl.ANY)] * 3,
-        out_specs=(VM,) * 7,
+        in_specs=[SM] + [VM] * 2 + [pl.BlockSpec(memory_space=pl.ANY)] * 6,
+        out_specs=(VM,) * 6,
         scratch_shapes=[
+            vm(*blocks), vm(*blocks), vm(*wt.shape),
             vm(*queries.shape), vm(*d_out.shape), vm(*inputs.shape),
+            vm(QB, PICKS, BLK, 2 * HD), vm(QB, RELAYS, BLK, 2 * HD), vm(QB, RELAYS, BLK, 2 * HD),
             vm(QB, PICKS, BLK, 2 * HD), vm(QB, PICKS + 1, BLK, 2 * HD), vf(RANKS, 8, HD),
             vm(QB, PICKS, BLK, 2 * HD), vf(RANKS, 8, HD),
             vf(OUTER, LOW, 8, HD), vf(LOW, 8, HD), vf(LOW, 8, HD),
@@ -441,14 +565,15 @@
             vm(RANKS * QB, HD), vm(RANKS * QB, HD), vm(HD, RANKS * QB), vm(HD, keys_all),
             vf(2, RANKS * QB, HD), vf(keys_all, 2 * HD), vf(HEADS, tokens), vf(QB, 4, 4 * BLK),
             dma(QB, PICKS), dma(QB, PICKS), dma(QB, PICKS), dma(QB, PICKS),
+            dma(QB, RELAYS), dma(QB, RELAYS), dma(QB, RELAYS), dma(QB, RELAYS),
             dma(LOW), dma(LOW), dma(OUTER), dma(OUTER),
-            dma(LOW), dma(LOW), dma(OUTER), dma(OUTER), dma(2), dma(2), dma(3),
+            dma(LOW), dma(LOW), dma(OUTER), dma(OUTER), dma(2), dma(2), dma(6),
         ],
         compiler_params=pltpu.CompilerParams(
-            collective_id=0, has_side_effects=True, vmem_limit_bytes=48 * MIB
+            collective_id=0, has_side_effects=True, vmem_limit_bytes=60 * MIB
         ),
     )(
-        sel, keys.reshape(blocks), values.reshape(blocks), comp_keys, comp_values, w2,
+        sel, comp_keys, comp_values, keys.reshape(blocks), values.reshape(blocks), wt,
         queries, d_out, inputs,
     )
 
@@ -462,11 +587,10 @@
             jax.ShapeDtypeStruct((QB, HD), BF),
             jax.ShapeDtypeStruct((tokens, half), BF),
         ),
-        in_specs=[SM] + [VM] * 7,
+        in_specs=[VM] * 6,
         out_specs=(VM,) * 5,
-        scratch_shapes=[pltpu.VMEM((QB, BLK, 2 * HD), F32)],
         compiler_params=pltpu.CompilerParams(vmem_limit_bytes=24 * MIB),
-    )(sel, back, down, csum, dz, dz_other, w2, w_other)
+    )(down, csum, dz, dz_other, wt, w_other)
     return dq, dk, dv, dck, dcv, dx
 
 

time: 135 us -> 118 us (0.87)
  Pallas kernels: 122 us -> 110 us
  local copies, waits for them, and re-layouts: 11.3 us -> 6.25 us
    pallas_call x1, Pallas kernels: 119 us -> 109 us  [body(): pl.pallas_call(attention_kernel, name='attention', out_shape=(jax.ShapeDt...]
    unnamed x18 -> x13, local copies, waits for them, and re-layouts: 10.2 us -> 6.25 us
    pallas_call x1, Pallas kernels: 3.03 us -> 1.36 us  [body(): pl.pallas_call(finish_kernel, name='finish', out_shape=(jax.ShapeDtypeStr...]
where the time goes in v3:
time: 118 us; the launch traced here: 117 us
  Pallas kernels  110 us (93%)
  local copies, waits for them, and re-layouts  6.25 us (5%)
    pallas_call x1, Pallas kernels, body(): pl.pallas_call(attention_kernel, name='attention', out_shape=(jax.ShapeDt...  109 us
    unnamed x13, local copies, waits for them, and re-layouts  6.25 us

profile of v3, /device:TPU:33, one launch (start us, length us, event | category | flops | bytes accessed | tf_op | source)
XLA Modules:
  0.0 117.3 jit_solution(5822130165374483182)
XLA Ops:
  0.6 0.0 copy-start
  0.6 109.0 %attention.1 = (bf16[256,2048]{1,0:T(8,128)(2,1)}, f32[4,64,256]{2,1,0:T(8,128)}, f32[8,128]{1,0:T(8,128)}, bf16[32,256]{1,0:T(8,128)(2,1)}, bf16[32,256]{1,0:T(8,128)(2,1)}, /*index=5*/bf16[32,1280]{1,0:T(8,128)(2,1)}) custom-call(s32[15,512]{1,0:T(8,128)} %bitcast.8, bf16[4,128]{1,0:T(4,128)(2,1)} %ck_ref.1, bf16[4,128]{1,0:T(4,128)(2,1)} %cv_ref.1, ...), custom_call_target="tpu_custom_call" | custom-call | tf_op jit(solution)/shard_map/attention/pallas_call | solution.py:543
  109.7 0.0 copy-done
  109.7 0.0 copy-start.1
  109.7 0.9 copy-done.1
  110.6 0.0 copy-start.2
  110.7 0.9 copy-done.2
  111.5 0.0 copy-start.3
  111.5 0.7 copy-done.3
  112.3 0.0 copy-start.4
  112.3 0.7 copy-done.4
  113.0 0.0 copy-start.5
  113.0 0.7 copy-done.5
  113.7 1.4 %finish.1 = (bf16[256,128]{1,0:T(8,128)(2,1)}, bf16[256,128]{1,0:T(8,128)(2,1)}, bf16[4,128]{1,0:T(4,128)(2,1)}, bf16[4,128]{1,0:T(4,128)(2,1)}, bf16[256,1280]{1,0:T(8,128)(2,1)}) custom-call(f32[4,64,256]{2,1,0:T(8,128)S(1)} %copy-done.1, f32[8,128]{1,0:T(8,128)S(1)} %copy-done.5, bf16[32,256]{1,0:T(8,128)(2,1)S(1)} %copy-done.3, ...), custom_call_target="tpu_custom_call" | custom-call | tf_op jit(solution)/shard_map/finish/pallas_call | solution.py:580
  115.0 2.3 %copy.16 = bf16[256,2048]{1,0:T(8,128)(2,1)} copy(bf16[256,2048]{1,0:T(8,128)(2,1)} %get-tuple-element.34) | data formatting | bytes 2097152
Async XLA Ops:
  0.6 109.1 %copy-start = (bf16[2560,32]{0,1:T(8,128)(2,1)S(1)}, bf16[2560,32]{0,1:T(8,128)(2,1)}, u32[]{:S(2)}) copy-start(bf16[2560,32]{0,1:T(8,128)(2,1)} %param.16) | copy-start | bytes 491524
  109.7 1.0 copy-start.1
  110.6 0.9 copy-start.2
  111.5 0.7 copy-start.3
  112.3 0.7 copy-start.4
  113.0 0.7 copy-start.5

commit v4 on v3

--- a/solution.py
+++ b/solution.py
@@ -13,7 +13,7 @@
 QB = 4
 RANKS = 128
 HEADS = 16
-LOW = 16
+LOW = 32
 OUTER = RANKS // LOW
 HALF = RANKS // 2
 PLANE = 32
@@ -80,19 +80,19 @@
 
 
 def reach_of(parity, j):
-    near = 1 + (j * (HALF - 1)) // (PICKS - 1)
-    far = HALF + 1 + (j * (HALF - 2)) // (PICKS - 1)
-    return jnp.where(parity == 0, near, far)
-
-
-def relayed(j, source, target):
-    odd = (j % 2 == 1) & (source // PLANE != target // PLANE)
-    return odd & (source % PLANE != target % PLANE)
-
-
-def stop(j, source, target):
-    relay = target // PLANE * PLANE + source % PLANE
-    return jnp.where(relayed(j, source, target), relay, target)
+    return jnp.where(parity == 0, 1 + ((j * 9) >> 1), HALF + 1 + ((j * 31 * 9363) >> 16))
+
+
+for _p, _j, _r in REACH:
+    assert _r == (1 + ((_j * 9) >> 1) if _p == 0 else HALF + 1 + ((_j * 31 * 9363) >> 16))
+
+
+def crosses(source, target):
+    return ((source >> 5) != (target >> 5)) & ((source & 31) != (target & 31))
+
+
+def stop(source, target):
+    return (target & ~31) | (source & 31)
 
 
 def each(n, visit):
@@ -105,20 +105,20 @@
 
 def attention_kernel(
     sel_ref, ck_ref, cv_ref, k_hbm, v_hbm, w_hbm, q_hbm, do_hbm, x_hbm,
-    dq_ref, down_ref, csum_ref, dz_ref, dzother_ref, wother_ref,
-    k_ref, v_ref, w_ref, q_ref, do_ref, x_ref, back_ref, relay_f, relay_b, out_buf, kv_ref, comp_ref, dkv_ref, dcomp_ref, b_buf, b_sum, a_buf,
+    dq_hbm, down_ref, csum_ref, dz_ref, dzother_ref, wother_ref,
+    dq_ref, k_ref, v_ref, w_ref, q_ref, do_ref, x_ref, back_ref, relay_f, relay_b, out_buf, kv_ref, comp_ref, dkv_ref, dcomp_ref, b_buf, b_sum, a_buf,
     doc, dos, dq_acc, bias_c, bias_s, ck, cv, ckt, kt, dc_acc, dkv_acc, delta_c, delta_s,
     kv_send, kv_recv, g_send, g_recv, f_send, f_recv, h_send, h_recv, a_send, a_recv, b_send, b_recv,
-    ra_send, ra_recv, rb_send, rb_recv, w_sems, z_sems, in_sems,
+    ra_send, ra_recv, rb_send, rb_recv, w_sems, z_sems, in_sems, dq_sems,
 ):
     me = lax.axis_index("ctx")
     hd = lax.axis_index("head")
-    group = me // LOW
-    low = me % LOW
+    group = me >> 5
+    low = me & 31
     partner = {"head": 1 - hd}
     tokens = q_ref.shape[0]
     half = w_ref.shape[1] // 2
-    place = me % PLANE
+    place = me & 31
 
     k_in = pltpu.make_async_copy(k_hbm, k_ref, in_sems.at[3])
     v_in = pltpu.make_async_copy(v_hbm, v_ref, in_sems.at[4])
@@ -147,10 +147,7 @@
         def _():
             signal(barrier, at_ctx(g * LOW + low))
 
-    @functools.partial(each, 2 * PICKS)
-    def _(n):
-        r = reach_of(n // PICKS, n % PICKS)
-
+    for p, j, r in REACH:
         @pl.when(me >= r)
         def _():
             signal(barrier, at_ctx(me - r))
@@ -161,32 +158,31 @@
 
     signal(barrier, partner)
 
-    comp_ref[pl.ds(me, 1), 0:4, :] = ck_ref[...].astype(F32)[None]
-    comp_ref[pl.ds(me, 1), 4:8, :] = cv_ref[...].astype(F32)[None]
+    own = jnp.concatenate([ck_ref[...].astype(F32), cv_ref[...].astype(F32)], axis=0)
+    comp_ref[pl.ds(me, 1)] = own.astype(BF)[None]
 
     @functools.partial(each, OUTER)
     def _(g):
         @pl.when(g > group)
         def _():
-            comp_ref[pl.ds(g * LOW, LOW)] = jnp.zeros((LOW, 8, HD), F32)
+            comp_ref[pl.ds(g * LOW, LOW)] = jnp.zeros((LOW, 8, HD), BF)
 
     k_in.wait()
     v_in.wait()
+    for p, j, r in REACH:
+        asker = jnp.minimum(me + r, RANKS - 1)
+        for i in range(2):
+            local = sel_ref[j, asker * QB + (p + 2 * i)] & (QB - 1)
+            out_buf[p, j, i, :, 0:HD] = k_ref[local]
+            out_buf[p, j, i, :, HD:] = v_ref[local]
+
+        @pl.when(me < r)
+        def _():
+            kv_ref[:, p, j] = jnp.zeros((2, BLK, 2 * HD), BF)
+
     for b in range(QB):
-        @functools.partial(each, PICKS)
-        def _(j):
-            r = reach_of(b % 2, j)
-            asker = jnp.minimum(me + r, RANKS - 1)
-            local = sel_ref[j, asker * QB + b] & (QB - 1)
-            out_buf[b, j, :, 0:HD] = k_ref[local]
-            out_buf[b, j, :, HD:] = v_ref[local]
-
-            @pl.when(me < r)
-            def _():
-                kv_ref[b, j] = jnp.zeros((BLK, 2 * HD), BF)
-
-        kv_ref[b, PICKS, :, 0:HD] = k_ref[b]
-        kv_ref[b, PICKS, :, HD:] = v_ref[b]
+        kv_ref[b // 2, b % 2, PICKS, :, 0:HD] = k_ref[b]
+        kv_ref[b // 2, b % 2, PICKS, :, HD:] = v_ref[b]
 
     peers = count(
         [me + r < RANKS for _, _, r in REACH] + [me >= r for _, _, r in REACH]
@@ -195,7 +191,7 @@
 
     def a_copy(a, slot):
         return remote(
-            comp_ref.at[slot], comp_ref.at[slot], a_send.at[a], a_recv.at[slot % LOW],
+            comp_ref.at[slot], comp_ref.at[slot], a_send.at[a], a_recv.at[slot & 31],
             at_ctx(group * LOW + a),
         )
 
@@ -206,21 +202,21 @@
             at_ctx(g * LOW + low),
         )
 
-    def relay_copy(b, j, target):
-        return remote(
-            out_buf.at[b, j], relay_f.at[b, j // 2], kv_send.at[b, j], f_recv.at[b, j // 2],
+    def relay_copy(p, i, target):
+        return remote(
+            out_buf.at[p, 2 * i + 1], relay_f.at[p, i], kv_send.at[p, 2 * i + 1], f_recv.at[p, i],
             at_ctx(target),
         )
 
-    def forward_copy(b, i, target):
-        return remote(
-            relay_f.at[b, i], kv_ref.at[b, 2 * i + 1], f_send.at[b, i],
-            kv_recv.at[b, 2 * i + 1], at_ctx(target),
+    def forward_copy(p, i, target):
+        return remote(
+            relay_f.at[p, i], kv_ref.at[:, p, 2 * i + 1], f_send.at[p, i],
+            kv_recv.at[p, 2 * i + 1], at_ctx(target),
         )
 
     def grad_relay_copy(b, j, target):
         return remote(
-            dkv_ref.at[b, j], relay_b.at[b, j // 2], g_send.at[b, j], h_recv.at[b, j // 2],
+            dkv_ref.at[b, j], relay_b.at[b, j >> 1], g_send.at[b, j], h_recv.at[b, j >> 1],
             at_ctx(target),
         )
 
@@ -230,9 +226,9 @@
             g_recv.at[b, 2 * i + 1], at_ctx(target),
         )
 
-    def kv_copy(b, j, target):
-        return remote(
-            out_buf.at[b, j], kv_ref.at[b, j], kv_send.at[b, j], kv_recv.at[b, j], at_ctx(target)
+    def kv_copy(p, j, target):
+        return remote(
+            out_buf.at[p, j], kv_ref.at[:, p, j], kv_send.at[p, j], kv_recv.at[p, j], at_ctx(target)
         )
 
     def grad_copy(b, j, target):
@@ -270,27 +266,17 @@
             def _():
                 visit(g)
 
-    def askers(b, visit):
-        @functools.partial(each, PICKS)
-        def _(j):
-            r = reach_of(b % 2, j)
-
-            @pl.when(me + r < RANKS)
-            def _():
-                visit(j, me + r)
-
     def owners(b, visit):
-        @functools.partial(each, PICKS)
-        def _(j):
-            r = reach_of(b % 2, j)
+        for j in range(PICKS):
+            r = jnp.where((b & 1) == 0, reach(0, j), reach(1, j))
 
             @pl.when(me >= r)
             def _():
                 visit(j, me - r)
 
-    def fetch_forwards(b, i, visit):
-        r = reach_of(b % 2, 2 * i + 1)
-        planes = (place + r) // PLANE
+    def fetch_forwards(p, i, visit):
+        r = reach_of(p, 2 * i + 1)
+        planes = (place + r) >> 5
         source = me - PLANE * planes
         target = source + r
 
@@ -299,8 +285,8 @@
             visit(target)
 
     def grad_forwards(b, i, visit):
-        r = reach_of(b % 2, 2 * i + 1)
-        planes = (r - place + PLANE - 1) // PLANE
+        r = reach_of(b & 1, 2 * i + 1)
+        planes = (r - place + PLANE - 1) >> 5
         source = me + PLANE * planes
         target = source - r
 
@@ -308,35 +294,35 @@
         def _():
             visit(target)
 
-    def send_relayed(b):
-        def visit(j, t):
-            @pl.when(relayed(j, me, t))
+    def send_relayed(q):
+        for p, j, r in REACH:
+            if p == q and j % 2 == 1 and r % PLANE != 0:
+                @pl.when((me + r < RANKS) & crosses(me, me + r))
+                def _():
+                    relay_copy(p, j // 2, stop(me, me + r)).start()
+
+    def send_direct(q):
+        for p, j, r in REACH[q * PICKS:(q + 1) * PICKS]:
+            inside = me + r < RANKS
+            if j % 2 == 1 and r % PLANE != 0:
+                inside = inside & jnp.logical_not(crosses(me, me + r))
+
+            @pl.when(inside)
             def _():
-                relay_copy(b, j, stop(j, me, t)).start()
-
-        askers(b, visit)
-
-    def send_direct(b):
-        def visit(j, t):
-            @pl.when(jnp.logical_not(relayed(j, me, t)))
-            def _():
-                kv_copy(b, j, t).start()
-
-        askers(b, visit)
+                kv_copy(p, j, me + r).start()
 
     others_low(lambda a: a_copy(a, me).start())
-    for b in range(QB):
-        send_relayed(b)
+    send_relayed(0)
     others_low(lambda a: a_copy(a, group * LOW + a).wait_recv())
     outer_where(lambda g: g > group, lambda g: b_copy(g, group).start())
-    for b in range(QB):
-        send_direct(b)
+    send_direct(0)
+    send_relayed(1)
     w_in.wait()
     w_copy.start()
 
     row = lax.broadcasted_iota(jnp.int32, (RANKS * QB, tokens), 0)
     col = lax.broadcasted_iota(jnp.int32, (RANKS * QB, tokens), 1)
-    bias_c[...] = jnp.where(row <= me * QB + col // BLK, 0.0, -jnp.inf)
+    bias_c[...] = jnp.where(row <= me * QB + (col >> 6), 0.0, -jnp.inf)
     srow = lax.broadcasted_iota(jnp.int32, (BLK, 4 * BLK), 0)
     scol = lax.broadcasted_iota(jnp.int32, (BLK, 4 * BLK), 1) % BLK
     own_bias = jnp.where(srow <= scol, 0.0, -jnp.inf)
@@ -356,7 +342,7 @@
     q_in.wait()
 
     outer_where(lambda g: g < group, lambda g: b_copy(g, g).wait_recv())
-    pairs = comp_ref[...].reshape(RANKS // 2, 2, 8, HD)
+    pairs = comp_ref[...].astype(F32).reshape(RANKS // 2, 2, 8, HD)
     even, odd = pairs[:, 0], pairs[:, 1]
     top_rows = lax.broadcasted_iota(jnp.int32, (RANKS // 2, 8, HD), 1) < 4
     swap = lambda z: pltpu.roll(z, 4, 1)
@@ -369,17 +355,20 @@
 
     @functools.partial(each, HEADS)
     def _(h):
-        @pl.when(h < QB * RELAYS // 2)
-        def _():
-            for i in range(2):
-                n = 2 * h + i
-                b, entry = n // RELAYS, n % RELAYS
-
-                def pass_on(target):
-                    relay_copy(b, 2 * entry + 1, target).wait_recv()
-                    forward_copy(b, entry, target).start()
-
-                fetch_forwards(b, entry, pass_on)
+        @pl.when(h < 2 * RELAYS)
+        def _():
+            p = (h >= RELAYS).astype(jnp.int32)
+            i = h - RELAYS * p
+
+            def pass_on(target):
+                relay_copy(p, i, target).wait_recv()
+                forward_copy(p, i, target).start()
+
+            fetch_forwards(p, i, pass_on)
+
+        @pl.when(h == 8)
+        def _():
+            send_direct(1)
 
         lanes = pl.ds(pl.multiple_of(h * HD, HD), HD)
         dqt, dk, dv, delta = scores_backward(
@@ -397,14 +386,33 @@
     ).reshape(RANKS, 8, HD)
     outer_where(lambda g: g < group, lambda g: rb_copy(g, group).start())
 
+    def dq_out(b):
+        rows = pl.ds(pl.multiple_of(b * BLK, BLK), BLK)
+        return pltpu.make_async_copy(dq_ref.at[rows], dq_hbm.at[rows], dq_sems.at[b])
+
     @functools.partial(each, QB)
     def _(b):
-        owners(b, lambda j, t: kv_copy(b, j, t).wait_recv())
+        @pl.when(b < 2)
+        def _():
+            owners(b, lambda j, t: kv_copy(b, j, t).wait_recv())
+
+        @pl.when(b == 2)
+        def _():
+            b_sum[...] = dcomp_ref[pl.ds(group * LOW, LOW)]
+
+            def add_outer(g):
+                rb_copy(g, g).wait_recv()
+                b_sum[...] += b_buf[g]
+
+            outer_where(lambda g: g > group, add_outer)
+            others_low(lambda a: ra_copy(a, low).start())
+            a_buf[pl.ds(low, 1)] = b_sum[pl.ds(low, 1)]
+
         rows = pl.ds(pl.multiple_of(b * BLK, BLK), BLK)
         keys_all = (PICKS + 1) * BLK
-        kt[...] = kv_ref[b, :, :, 0:HD].reshape(keys_all, HD).astype(F32).T.astype(BF)
+        kt[...] = kv_ref[b >> 1, b & 1, :, :, 0:HD].reshape(keys_all, HD).astype(F32).T.astype(BF)
         dkv_acc[...] = jnp.zeros_like(dkv_acc)
-        bias = bias_s.at[b % 2]
+        bias = bias_s.at[b & 1]
 
         @functools.partial(each, 4)
         def _(g):
@@ -412,8 +420,8 @@
             q = jnp.concatenate([q_ref[rows, l] for l in lanes], axis=0)
             do = jnp.concatenate([dos[rows, l] for l in lanes], axis=0)
             dqt, dk, dv, delta = scores_backward(
-                kv_ref[b, :, :, 0:HD].reshape(keys_all, HD),
-                kv_ref[b, :, :, HD:].reshape(keys_all, HD),
+                kv_ref[b >> 1, b & 1, :, :, 0:HD].reshape(keys_all, HD),
+                kv_ref[b >> 1, b & 1, :, :, HD:].reshape(keys_all, HD),
                 kt[...], bias[...], q, do,
             )
             dq = dqt.T
@@ -432,17 +440,21 @@
         down_ref[b] = total[PICKS * BLK:]
 
         def send_grad(j, t):
-            hop = relayed(j, me, t) & (b < QB - 1)
-
-            @pl.when(hop)
-            def _():
-                grad_relay_copy(b, j, stop(j, me, t)).start()
-
-            @pl.when(jnp.logical_not(hop))
-            def _():
+            if j % 2 == 0:
                 grad_copy(b, j, t).start()
+            else:
+                hop = crosses(me, t) & (b < QB - 1)
+
+                @pl.when(hop)
+                def _():
+                    grad_relay_copy(b, j, stop(me, t)).start()
+
+                @pl.when(jnp.logical_not(hop))
+                def _():
+                    grad_copy(b, j, t).start()
 
         owners(b, send_grad)
+        dq_out(b).start()
 
         @pl.when(b > 0)
         def _():
@@ -465,41 +477,43 @@
     dz_ref[HEADS:, :] = (sel * (1.0 - gate_t[HEADS:])).astype(BF)
     z_copy.start()
 
-    b_sum[...] = dcomp_ref[pl.ds(group * LOW, LOW)]
-
-    def add_outer(g):
-        rb_copy(g, g).wait_recv()
-        b_sum[...] += b_buf[g]
-
-    outer_where(lambda g: g > group, add_outer)
-    others_low(lambda a: ra_copy(a, low).start())
-    a_buf[pl.ds(low, 1)] = b_sum[pl.ds(low, 1)]
-
-    def add_arrived(b):
-        def visit(j, t):
-            grad_copy(b, j, t).wait_recv()
-            local = sel_ref[j, t * QB + b] & (QB - 1)
-            term = back_ref[b, j].astype(F32)
-            for c in range(QB):
-                down_ref[c] += jnp.where(local == c, term, 0.0)
-
-        askers(b, visit)
-
     for b in range(QB):
-        add_arrived(b)
+        @functools.partial(each, PICKS)
+        def _(j):
+            t = me + reach_of(b & 1, j)
+
+            @pl.when(t < RANKS)
+            def _():
+                grad_copy(b, j, t).wait_recv()
+                local = sel_ref[j, t * QB + b] & (QB - 1)
+                term = back_ref[b, j].astype(F32)
+                for c in range(QB):
+                    down_ref[c] += jnp.where(local == c, term, 0.0)
+
     others_low(lambda a: ra_copy(a, a).wait_recv())
     csum_ref[...] = jnp.sum(a_buf[...], axis=0)
     w_copy.wait_recv()
     z_copy.wait_recv()
-    for b in range(QB):
-        askers(b, lambda j, t: kv_copy(b, j, t).wait_send())
-        owners(b, lambda j, t: grad_copy(b, j, t).wait_send())
-
+    each(QB, lambda b: dq_out(b).wait())
+    for p, j, r in REACH:
+        @pl.when(me + r < RANKS)
+        def _():
+            kv_copy(p, j, me + r).wait_send()
+
+    for p in range(2):
         @functools.partial(each, RELAYS)
         def _(i):
-            fetch_forwards(b, i, lambda t: forward_copy(b, i, t).wait_send())
-            if b < QB - 1:
-                grad_forwards(b, i, lambda t: grad_forward_copy(b, i, t).wait_send())
+            fetch_forwards(p, i, lambda t: forward_copy(p, i, t).wait_send())
+
+    @functools.partial(each, QB)
+    def _(b):
+        owners(b, lambda j, t: grad_copy(b, j, t).wait_send())
+
+    @functools.partial(each, QB - 1)
+    def _(b):
+        @functools.partial(each, RELAYS)
+        def _(i):
+            grad_forwards(b, i, lambda t: grad_forward_copy(b, i, t).wait_send())
 
     others_low(lambda a: a_copy(a, me).wait_send())
     outer_where(lambda g: g > group, lambda g: b_copy(g, group).wait_send())
@@ -510,18 +524,31 @@
 
 
 def finish_kernel(
-    down_ref, csum_ref, dz_ref, dzother_ref, w_ref, wother_ref, dk_ref, dv_ref, dck_ref, dcv_ref, dx_ref
+    dq_hbm, down_hbm, csum_hbm, dz_hbm, dzother_hbm, w_hbm, wother_hbm,
+    dqo_ref, dk_ref, dv_ref, dck_ref, dcv_ref, dx_ref,
+    down_ref, csum_ref, dz_ref, dzother_ref, w_ref, wother_ref, sems,
 ):
     hd = lax.axis_index("head")
     half = wother_ref.shape[1]
     mine = pl.ds(pl.multiple_of(hd * half, HD), half)
+    pairs = [
+        (dz_hbm, dz_ref), (dzother_hbm, dzother_ref), (w_hbm.at[:, mine], w_ref),
+        (wother_hbm, wother_ref), (down_hbm, down_ref), (csum_hbm, csum_ref), (dq_hbm, dqo_ref),
+    ]
+    copies = [pltpu.make_async_copy(a, c, sems.at[i]) for i, (a, c) in enumerate(pairs)]
+    copies[-1].start()
+    for copy in copies[:-1]:
+        copy.start()
+    for copy in copies[:-1]:
+        copy.wait()
     for b in range(QB):
         dk_ref[b * BLK:(b + 1) * BLK, :] = down_ref[b, :, 0:HD].astype(BF)
         dv_ref[b * BLK:(b + 1) * BLK, :] = down_ref[b, :, HD:].astype(BF)
     dck_ref[...] = csum_ref[0:4, :].astype(BF)
     dcv_ref[...] = csum_ref[4:8, :].astype(BF)
     tn = lambda a, c: lax.dot_general(a, c, (((0,), (0,)), ((), ())), preferred_element_type=F32)
-    dx_ref[...] = (tn(dz_ref[...], w_ref[:, mine]) + tn(dzother_ref[...], wother_ref[...])).astype(BF)
+    dx_ref[...] = (tn(dz_ref[...], w_ref[...]) + tn(dzother_ref[...], wother_ref[...])).astype(BF)
+    copies[-1].wait()
 
 
 VM = pl.BlockSpec(memory_space=pltpu.VMEM)
@@ -552,22 +579,24 @@
             jax.ShapeDtypeStruct((2 * HEADS, half), BF),
         ),
         in_specs=[SM] + [VM] * 2 + [pl.BlockSpec(memory_space=pl.ANY)] * 6,
-        out_specs=(VM,) * 6,
+        out_specs=(pl.BlockSpec(memory_space=pl.ANY),) + (VM,) * 5,
         scratch_shapes=[
+            vm(*queries.shape),
             vm(*blocks), vm(*blocks), vm(*wt.shape),
             vm(*queries.shape), vm(*d_out.shape), vm(*inputs.shape),
-            vm(QB, PICKS, BLK, 2 * HD), vm(QB, RELAYS, BLK, 2 * HD), vm(QB, RELAYS, BLK, 2 * HD),
-            vm(QB, PICKS, BLK, 2 * HD), vm(QB, PICKS + 1, BLK, 2 * HD), vf(RANKS, 8, HD),
+            vm(QB, PICKS, BLK, 2 * HD),
+            vm(2, RELAYS, 2, BLK, 2 * HD), vm(QB - 1, RELAYS, BLK, 2 * HD),
+            vm(2, PICKS, 2, BLK, 2 * HD), vm(2, 2, PICKS + 1, BLK, 2 * HD), vm(RANKS, 8, HD),
             vm(QB, PICKS, BLK, 2 * HD), vf(RANKS, 8, HD),
             vf(OUTER, LOW, 8, HD), vf(LOW, 8, HD), vf(LOW, 8, HD),
             vm(*queries.shape), vm(*queries.shape), vf(*queries.shape),
             vf(RANKS * QB, tokens), vf(2, keys_all, 4 * BLK),
             vm(RANKS * QB, HD), vm(RANKS * QB, HD), vm(HD, RANKS * QB), vm(HD, keys_all),
             vf(2, RANKS * QB, HD), vf(keys_all, 2 * HD), vf(HEADS, tokens), vf(QB, 4, 4 * BLK),
-            dma(QB, PICKS), dma(QB, PICKS), dma(QB, PICKS), dma(QB, PICKS),
-            dma(QB, RELAYS), dma(QB, RELAYS), dma(QB, RELAYS), dma(QB, RELAYS),
+            dma(2, PICKS), dma(2, PICKS), dma(QB, PICKS), dma(QB, PICKS),
+            dma(2, RELAYS), dma(2, RELAYS), dma(QB - 1, RELAYS), dma(QB - 1, RELAYS),
             dma(LOW), dma(LOW), dma(OUTER), dma(OUTER),
-            dma(LOW), dma(LOW), dma(OUTER), dma(OUTER), dma(2), dma(2), dma(6),
+            dma(LOW), dma(LOW), dma(OUTER), dma(OUTER), dma(2), dma(2), dma(6), dma(QB),
         ],
         compiler_params=pltpu.CompilerParams(
             collective_id=0, has_side_effects=True, vmem_limit_bytes=60 * MIB
@@ -577,21 +606,26 @@
         queries, d_out, inputs,
     )
 
-    dk, dv, dck, dcv, dx = pl.pallas_call(
+    any_space = pl.BlockSpec(memory_space=pl.ANY)
+    return pl.pallas_call(
         finish_kernel,
         name="finish",
         out_shape=(
+            jax.ShapeDtypeStruct(queries.shape, BF),
             jax.ShapeDtypeStruct((tokens, HD), BF),
             jax.ShapeDtypeStruct((tokens, HD), BF),
             jax.ShapeDtypeStruct((QB, HD), BF),
             jax.ShapeDtypeStruct((QB, HD), BF),
             jax.ShapeDtypeStruct((tokens, half), BF),
         ),
-        in_specs=[VM] * 6,
-        out_specs=(VM,) * 5,
-        compiler_params=pltpu.CompilerParams(vmem_limit_bytes=24 * MIB),
-    )(down, csum, dz, dz_other, wt, w_other)
-    return dq, dk, dv, dck, dcv, dx
+        in_specs=[any_space] * 7,
+        out_specs=(VM,) * 6,
+        scratch_shapes=[
+            vf(QB, BLK, 2 * HD), vf(8, HD), vm(2 * HEADS, tokens), vm(2 * HEADS, tokens),
+            vm(2 * HEADS, half), vm(2 * HEADS, half), dma(7),
+        ],
+        compiler_params=pltpu.CompilerParams(vmem_limit_bytes=60 * MIB),
+    )(dq, down, csum, dz, dz_other, wt, w_other)
 
 
 def solution(mesh):

time: 118 us -> 99.2 us (0.84)
  Pallas kernels: 110 us -> 98.1 us
  local copies, waits for them, and re-layouts: 6.25 us -> 0 us
    pallas_call x1, Pallas kernels: 109 us -> 94.9 us  [body(): pl.pallas_call(attention_kernel, name='attention', out_shape=(jax.ShapeDt...]
    unnamed x13 -> x0, local copies, waits for them, and re-layouts: 6.25 us -> none
    pallas_call x1, Pallas kernels: 1.36 us -> 3.18 us  [body(): pl.pallas_call(finish_kernel, name='finish', out_shape=(jax.ShapeDtypeStr...]
where the time goes in v4:
time: 99.2 us; the launch traced here: 98.7 us
  Pallas kernels  98.1 us (99%)
    pallas_call x1, Pallas kernels, body(): pl.pallas_call(attention_kernel, name='attention', out_shape=(jax.ShapeDt...  94.9 us
    pallas_call x1, Pallas kernels, body(): pl.pallas_call(finish_kernel, name='finish', out_shape=(jax.ShapeDtypeStr...  3.18 us

profile of v4, /device:TPU:33, one launch (start us, length us, event | category | flops | bytes accessed | tf_op | source)
XLA Modules:
  0.0 98.7 jit_solution(8239534050231988268)
XLA Ops:
  0.6 94.9 %attention.1 = (bf16[256,2048]{1,0:T(8,128)(2,1)}, f32[4,64,256]{2,1,0:T(8,128)}, f32[8,128]{1,0:T(8,128)}, bf16[32,256]{1,0:T(8,128)(2,1)}, bf16[32,256]{1,0:T(8,128)(2,1)}, /*index=5*/bf16[32,1280]{1,0:T(8,128)(2,1)}) custom-call(s32[15,512]{1,0:T(8,128)} %bitcast.8, bf16[4,128]{1,0:T(4,128)(2,1)} %ck_ref.1, bf16[4,128]{1,0:T(4,128)(2,1)} %cv_ref.1, ...), custom_call_target="tpu_custom_call" | custom-call | tf_op jit(solution)/shard_map/attention/pallas_call | solution.py:570
  95.6 3.2 %finish.1 = (bf16[256,2048]{1,0:T(8,128)(2,1)}, bf16[256,128]{1,0:T(8,128)(2,1)}, bf16[256,128]{1,0:T(8,128)(2,1)}, bf16[4,128]{1,0:T(4,128)(2,1)}, bf16[4,128]{1,0:T(4,128)(2,1)}, /*index=5*/bf16[256,1280]{1,0:T(8,128)(2,1)}) custom-call(bf16[256,2048]{1,0:T(8,128)(2,1)} %get-tuple-element.12.dq_hbm, f32[4,64,256]{2,1,0:T(8,128)} %get-tuple-element.13.down_hbm, ...), custom_call_target="tpu_custom_call" | custom-call | tf_op jit(solution)/shard_map/finish/pallas_call | solution.py:610

commit v5 on v4

--- a/solution.py
+++ b/solution.py
@@ -65,18 +65,21 @@
     return lax.dot_general(a, b, (((1,), (0,)), ((), ())), preferred_element_type=F32)
 
 
-def scores_backward(k, v, kt, bias, q, do):
-    s = nt(k, q) * (SCALE * LOG2E) + bias
-    top = jnp.max(s, axis=0, keepdims=True)
-    e = jnp.exp2(s - top)
-    prob = e * (1.0 / jnp.sum(e, axis=0, keepdims=True))
-    dp = nt(v, do)
-    delta = jnp.sum(prob * dp, axis=0, keepdims=True)
-    ds = (prob * (dp - delta)).astype(BF)
-    dv = nn(prob.astype(BF), do)
-    dk = nn(ds, q)
-    dqt = nn(kt, ds)
-    return dqt, dk, dv, delta
+def scores_backward(k, v, kt, bias, pairs):
+    s = [nt(k, q) * (SCALE * LOG2E) + bias for q, _ in pairs]
+    dp = [nt(v, do) for _, do in pairs]
+    outs = []
+    for i, (q, do) in enumerate(pairs):
+        top = jnp.max(s[i], axis=0, keepdims=True)
+        e = jnp.exp2(s[i] - top)
+        prob = e * (1.0 / jnp.sum(e, axis=0, keepdims=True))
+        delta = jnp.sum(prob * dp[i], axis=0, keepdims=True)
+        ds = (prob * (dp[i] - delta)).astype(BF)
+        dv = nn(prob.astype(BF), do)
+        dk = nn(ds, q)
+        dqt = nn(kt, ds)
+        outs.append((dqt, dk, dv, delta))
+    return outs
 
 
 def reach_of(parity, j):
@@ -161,29 +164,6 @@
     own = jnp.concatenate([ck_ref[...].astype(F32), cv_ref[...].astype(F32)], axis=0)
     comp_ref[pl.ds(me, 1)] = own.astype(BF)[None]
 
-    @functools.partial(each, OUTER)
-    def _(g):
-        @pl.when(g > group)
-        def _():
-            comp_ref[pl.ds(g * LOW, LOW)] = jnp.zeros((LOW, 8, HD), BF)
-
-    k_in.wait()
-    v_in.wait()
-    for p, j, r in REACH:
-        asker = jnp.minimum(me + r, RANKS - 1)
-        for i in range(2):
-            local = sel_ref[j, asker * QB + (p + 2 * i)] & (QB - 1)
-            out_buf[p, j, i, :, 0:HD] = k_ref[local]
-            out_buf[p, j, i, :, HD:] = v_ref[local]
-
-        @pl.when(me < r)
-        def _():
-            kv_ref[:, p, j] = jnp.zeros((2, BLK, 2 * HD), BF)
-
-    for b in range(QB):
-        kv_ref[b // 2, b % 2, PICKS, :, 0:HD] = k_ref[b]
-        kv_ref[b // 2, b % 2, PICKS, :, HD:] = v_ref[b]
-
     peers = count(
         [me + r < RANKS for _, _, r in REACH] + [me >= r for _, _, r in REACH]
     )
@@ -312,10 +292,36 @@
                 kv_copy(p, j, me + r).start()
 
     others_low(lambda a: a_copy(a, me).start())
+    @functools.partial(each, OUTER)
+    def _(g):
+        @pl.when(g > group)
+        def _():
+            comp_ref[pl.ds(g * LOW, LOW)] = jnp.zeros((LOW, 8, HD), BF)
+
+    k_in.wait()
+    v_in.wait()
+    def prepare(q):
+        for p, j, r in REACH[q * PICKS:(q + 1) * PICKS]:
+            asker = jnp.minimum(me + r, RANKS - 1)
+            for i in range(2):
+                local = sel_ref[j, asker * QB + (p + 2 * i)] & (QB - 1)
+                out_buf[p, j, i, :, 0:HD] = k_ref[local]
+                out_buf[p, j, i, :, HD:] = v_ref[local]
+
+            @pl.when(me < r)
+            def _():
+                kv_ref[:, p, j] = jnp.zeros((2, BLK, 2 * HD), BF)
+
+    for b in range(QB):
+        kv_ref[b // 2, b % 2, PICKS, :, 0:HD] = k_ref[b]
+        kv_ref[b // 2, b % 2, PICKS, :, HD:] = v_ref[b]
+
+    prepare(0)
     send_relayed(0)
     others_low(lambda a: a_copy(a, group * LOW + a).wait_recv())
     outer_where(lambda g: g > group, lambda g: b_copy(g, group).start())
     send_direct(0)
+    prepare(1)
     send_relayed(1)
     w_in.wait()
     w_copy.start()
@@ -353,31 +359,34 @@
     ckt[...] = keys_c.T.astype(BF)
     dc_acc[...] = jnp.zeros_like(dc_acc)
 
-    @functools.partial(each, HEADS)
-    def _(h):
-        @pl.when(h < 2 * RELAYS)
-        def _():
-            p = (h >= RELAYS).astype(jnp.int32)
-            i = h - RELAYS * p
-
-            def pass_on(target):
-                relay_copy(p, i, target).wait_recv()
-                forward_copy(p, i, target).start()
-
-            fetch_forwards(p, i, pass_on)
-
-        @pl.when(h == 8)
+    @functools.partial(each, HEADS // 2)
+    def _(h2):
+        @pl.when(h2 < RELAYS)
+        def _():
+            for n in range(2):
+                h = 2 * h2 + n
+                p = (h >= RELAYS).astype(jnp.int32)
+                i = h - RELAYS * p
+
+                def pass_on(target):
+                    relay_copy(p, i, target).wait_recv()
+                    forward_copy(p, i, target).start()
+
+                fetch_forwards(p, i, pass_on)
+
+        @pl.when(h2 == 4)
         def _():
             send_direct(1)
 
-        lanes = pl.ds(pl.multiple_of(h * HD, HD), HD)
-        dqt, dk, dv, delta = scores_backward(
-            ck[...], cv[...], ckt[...], bias_c[...], q_ref[:, lanes], doc[:, lanes]
-        )
-        dq_acc[:, lanes] = dqt.T
-        dc_acc[0] += dk
-        dc_acc[1] += dv
-        delta_c[pl.ds(h, 1), :] = delta
+        heads = [pl.ds(pl.multiple_of((2 * h2 + i) * HD, HD), HD) for i in range(2)]
+        outs = scores_backward(
+            ck[...], cv[...], ckt[...], bias_c[...], [(q_ref[:, l], doc[:, l]) for l in heads]
+        )
+        for i in range(2):
+            dq_acc[:, heads[i]] = outs[i][0].T
+            delta_c[pl.ds(2 * h2 + i, 1), :] = outs[i][3]
+        dc_acc[0] += outs[0][1] + outs[1][1]
+        dc_acc[1] += outs[0][2] + outs[1][2]
 
     dck = (dc_acc[0] * SCALE).reshape(RANKS // 2, 8, HD)
     dcv = dc_acc[1].reshape(RANKS // 2, 8, HD)
@@ -390,13 +399,25 @@
         rows = pl.ds(pl.multiple_of(b * BLK, BLK), BLK)
         return pltpu.make_async_copy(dq_ref.at[rows], dq_hbm.at[rows], dq_sems.at[b])
 
+    def pass_grads(b):
+        @functools.partial(each, RELAYS)
+        def _(i):
+            def pass_on(target):
+                grad_relay_copy(b, 2 * i + 1, target).wait_recv()
+                grad_forward_copy(b, i, target).start()
+
+            grad_forwards(b, i, pass_on)
+
     @functools.partial(each, QB)
-    def _(b):
-        @pl.when(b < 2)
-        def _():
-            owners(b, lambda j, t: kv_copy(b, j, t).wait_recv())
-
-        @pl.when(b == 2)
+    def _(turn):
+        b = ((turn & 1) << 1) | (turn >> 1)
+        last = ((turn - 1) & 1) << 1 | ((turn - 1) >> 1)
+
+        @pl.when((turn & 1) == 0)
+        def _():
+            owners(b, lambda j, t: kv_copy(turn >> 1, j, t).wait_recv())
+
+        @pl.when(turn == 2)
         def _():
             b_sum[...] = dcomp_ref[pl.ds(group * LOW, LOW)]
 
@@ -414,23 +435,24 @@
         dkv_acc[...] = jnp.zeros_like(dkv_acc)
         bias = bias_s.at[b & 1]
 
-        @functools.partial(each, 4)
-        def _(g):
-            lanes = [pl.ds(pl.multiple_of((g + 4 * i) * HD, HD), HD) for i in range(4)]
-            q = jnp.concatenate([q_ref[rows, l] for l in lanes], axis=0)
-            do = jnp.concatenate([dos[rows, l] for l in lanes], axis=0)
-            dqt, dk, dv, delta = scores_backward(
+        @functools.partial(each, 2)
+        def _(g2):
+            groups = [2 * g2, 2 * g2 + 1]
+            lanes = [[pl.ds(pl.multiple_of((g + 4 * i) * HD, HD), HD) for i in range(4)] for g in groups]
+            stack = lambda ref, ls: jnp.concatenate([ref[rows, l] for l in ls], axis=0)
+            outs = scores_backward(
                 kv_ref[b >> 1, b & 1, :, :, 0:HD].reshape(keys_all, HD),
                 kv_ref[b >> 1, b & 1, :, :, HD:].reshape(keys_all, HD),
-                kt[...], bias[...], q, do,
+                kt[...], bias[...], [(stack(q_ref, ls), stack(dos, ls)) for ls in lanes],
             )
-            dq = dqt.T
-            for i in range(4):
-                total = (dq[i * BLK:(i + 1) * BLK] + dq_acc[rows, lanes[i]]) * SCALE
-                dq_ref[rows, lanes[i]] = total.astype(BF)
-            dkv_acc[:, 0:HD] += dk
-            dkv_acc[:, HD:] += dv
-            delta_s[b, pl.ds(g, 1), :] = delta
+            for n in range(2):
+                dq = outs[n][0].T
+                for i in range(4):
+                    total = (dq[i * BLK:(i + 1) * BLK] + dq_acc[rows, lanes[n][i]]) * SCALE
+                    dq_ref[rows, lanes[n][i]] = total.astype(BF)
+                delta_s[b, pl.ds(groups[n], 1), :] = outs[n][3]
+            dkv_acc[:, 0:HD] += outs[0][1] + outs[1][1]
+            dkv_acc[:, HD:] += outs[0][2] + outs[1][2]
 
         factor = jnp.where(
             lax.broadcasted_iota(jnp.int32, (1, 2 * HD), 1) < HD, jnp.float32(SCALE), 1.0
@@ -443,7 +465,7 @@
             if j % 2 == 0:
                 grad_copy(b, j, t).start()
             else:
-                hop = crosses(me, t) & (b < QB - 1)
+                hop = crosses(me, t)
 
                 @pl.when(hop)
                 def _():
@@ -456,15 +478,9 @@
         owners(b, send_grad)
         dq_out(b).start()
 
-        @pl.when(b > 0)
-        def _():
-            @functools.partial(each, RELAYS)
-            def _(i):
-                def pass_on(target):
-                    grad_relay_copy(b - 1, 2 * i + 1, target).wait_recv()
-                    grad_forward_copy(b - 1, i, target).start()
-
-                grad_forwards(b - 1, i, pass_on)
+        @pl.when(turn > 0)
+        def _():
+            pass_grads(last)
 
     gate_t = jax.nn.sigmoid(nt(w_ref[...], x_ref[...]))
     dz_ref[0:HEADS, :] = (delta_c[...] * (1.0 - gate_t[0:HEADS])).astype(BF)
@@ -476,8 +492,9 @@
     sel = jnp.concatenate(columns, axis=1)
     dz_ref[HEADS:, :] = (sel * (1.0 - gate_t[HEADS:])).astype(BF)
     z_copy.start()
-
-    for b in range(QB):
+    pass_grads(QB - 1)
+
+    for b in (0, 2, 1, 3):
         @functools.partial(each, PICKS)
         def _(j):
             t = me + reach_of(b & 1, j)
@@ -509,7 +526,7 @@
     def _(b):
         owners(b, lambda j, t: grad_copy(b, j, t).wait_send())
 
-    @functools.partial(each, QB - 1)
+    @functools.partial(each, QB)
     def _(b):
         @functools.partial(each, RELAYS)
         def _(i):
@@ -585,7 +602,7 @@
             vm(*blocks), vm(*blocks), vm(*wt.shape),
             vm(*queries.shape), vm(*d_out.shape), vm(*inputs.shape),
             vm(QB, PICKS, BLK, 2 * HD),
-            vm(2, RELAYS, 2, BLK, 2 * HD), vm(QB - 1, RELAYS, BLK, 2 * HD),
+            vm(2, RELAYS, 2, BLK, 2 * HD), vm(QB, RELAYS, BLK, 2 * HD),
             vm(2, PICKS, 2, BLK, 2 * HD), vm(2, 2, PICKS + 1, BLK, 2 * HD), vm(RANKS, 8, HD),
             vm(QB, PICKS, BLK, 2 * HD), vf(RANKS, 8, HD),
             vf(OUTER, LOW, 8, HD), vf(LOW, 8, HD), vf(LOW, 8, HD),
@@ -594,7 +611,7 @@
             vm(RANKS * QB, HD), vm(RANKS * QB, HD), vm(HD, RANKS * QB), vm(HD, keys_all),
             vf(2, RANKS * QB, HD), vf(keys_all, 2 * HD), vf(HEADS, tokens), vf(QB, 4, 4 * BLK),
             dma(2, PICKS), dma(2, PICKS), dma(QB, PICKS), dma(QB, PICKS),
-            dma(2, RELAYS), dma(2, RELAYS), dma(QB - 1, RELAYS), dma(QB - 1, RELAYS),
+            dma(2, RELAYS), dma(2, RELAYS), dma(QB, RELAYS), dma(QB, RELAYS),
             dma(LOW), dma(LOW), dma(OUTER), dma(OUTER),
             dma(LOW), dma(LOW), dma(OUTER), dma(OUTER), dma(2), dma(2), dma(6), dma(QB),
         ],

time: 99.2 us -> 96.4 us (0.972)
  the two profiles are of different devices: /device:TPU:33 before, /device:TPU:17 now
where the time goes in v5:
time: 96.4 us; the launch traced here: 96.2 us
  Pallas kernels  95.5 us (99%)
    pallas_call x1, Pallas kernels, body(): pl.pallas_call(attention_kernel, name='attention', out_shape=(jax.ShapeDt...  92.4 us
    pallas_call x1, Pallas kernels, body(): pl.pallas_call(finish_kernel, name='finish', out_shape=(jax.ShapeDtypeStr...  3.18 us

profile of v5, /device:TPU:17, one launch (start us, length us, event | category | flops | bytes accessed | tf_op | source)
XLA Modules:
  0.0 96.2 jit_solution(10742853288203586725)
XLA Ops:
  0.6 92.4 %attention.1 = (bf16[256,2048]{1,0:T(8,128)(2,1)}, f32[4,64,256]{2,1,0:T(8,128)}, f32[8,128]{1,0:T(8,128)}, bf16[32,256]{1,0:T(8,128)(2,1)}, bf16[32,256]{1,0:T(8,128)(2,1)}, /*index=5*/bf16[32,1280]{1,0:T(8,128)(2,1)}) custom-call(s32[15,512]{1,0:T(8,128)} %bitcast.8, bf16[4,128]{1,0:T(4,128)(2,1)} %ck_ref.1, bf16[4,128]{1,0:T(4,128)(2,1)} %cv_ref.1, ...), custom_call_target="tpu_custom_call" | custom-call | tf_op jit(solution)/shard_map/attention/pallas_call | solution.py:587
  93.0 3.2 %finish.1 = (bf16[256,2048]{1,0:T(8,128)(2,1)}, bf16[256,128]{1,0:T(8,128)(2,1)}, bf16[256,128]{1,0:T(8,128)(2,1)}, bf16[4,128]{1,0:T(4,128)(2,1)}, bf16[4,128]{1,0:T(4,128)(2,1)}, /*index=5*/bf16[256,1280]{1,0:T(8,128)(2,1)}) custom-call(bf16[256,2048]{1,0:T(8,128)(2,1)} %get-tuple-element.12.dq_hbm, f32[4,64,256]{2,1,0:T(8,128)} %get-tuple-element.13.down_hbm, ...), custom_call_target="tpu_custom_call" | custom-call | tf_op jit(solution)/shard_map/finish/pallas_call | solution.py:627

commit v6 on v5

--- a/solution.py
+++ b/solution.py
@@ -361,18 +361,24 @@
 
     @functools.partial(each, HEADS // 2)
     def _(h2):
-        @pl.when(h2 < RELAYS)
+        def pass_keys(p, i):
+            def pass_on(target):
+                relay_copy(p, i, target).wait_recv()
+                forward_copy(p, i, target).start()
+
+            @pl.when(i < RELAYS)
+            def _():
+                fetch_forwards(p, i, pass_on)
+
+        @pl.when(h2 < 2)
+        def _():
+            for n in range(4):
+                pass_keys(0, 4 * h2 + n)
+
+        @pl.when(h2 >= 4)
         def _():
             for n in range(2):
-                h = 2 * h2 + n
-                p = (h >= RELAYS).astype(jnp.int32)
-                i = h - RELAYS * p
-
-                def pass_on(target):
-                    relay_copy(p, i, target).wait_recv()
-                    forward_copy(p, i, target).start()
-
-                fetch_forwards(p, i, pass_on)
+                pass_keys(1, 2 * (h2 - 4) + n)
 
         @pl.when(h2 == 4)
         def _():

time: 96.4 us -> 94.8 us (0.983)
  the two profiles are of different devices: /device:TPU:17 before, /device:TPU:33 now
where the time goes in v6:
time: 94.8 us; the launch traced here: 93.5 us
  Pallas kernels  92.8 us (98%)
    pallas_call x1, Pallas kernels, body(): pl.pallas_call(attention_kernel, name='attention', out_shape=(jax.ShapeDt...  89.7 us
    pallas_call x1, Pallas kernels, body(): pl.pallas_call(finish_kernel, name='finish', out_shape=(jax.ShapeDtypeStr...  3.18 us

profile of v6, /device:TPU:33, one launch (start us, length us, event | category | flops | bytes accessed | tf_op | source)
XLA Modules:
  0.0 93.5 jit_solution(1103818067991603826)
XLA Ops:
  0.6 89.7 %attention.1 = (bf16[256,2048]{1,0:T(8,128)(2,1)}, f32[4,64,256]{2,1,0:T(8,128)}, f32[8,128]{1,0:T(8,128)}, bf16[32,256]{1,0:T(8,128)(2,1)}, bf16[32,256]{1,0:T(8,128)(2,1)}, /*index=5*/bf16[32,1280]{1,0:T(8,128)(2,1)}) custom-call(s32[15,512]{1,0:T(8,128)} %bitcast.8, bf16[4,128]{1,0:T(4,128)(2,1)} %ck_ref.1, bf16[4,128]{1,0:T(4,128)(2,1)} %cv_ref.1, ...), custom_call_target="tpu_custom_call" | custom-call | tf_op jit(solution)/shard_map/attention/pallas_call | solution.py:593
  90.3 3.2 %finish.1 = (bf16[256,2048]{1,0:T(8,128)(2,1)}, bf16[256,128]{1,0:T(8,128)(2,1)}, bf16[256,128]{1,0:T(8,128)(2,1)}, bf16[4,128]{1,0:T(4,128)(2,1)}, bf16[4,128]{1,0:T(4,128)(2,1)}, /*index=5*/bf16[256,1280]{1,0:T(8,128)(2,1)}) custom-call(bf16[256,2048]{1,0:T(8,128)(2,1)} %get-tuple-element.12.dq_hbm, f32[4,64,256]{2,1,0:T(8,128)} %get-tuple-element.13.down_hbm, ...), custom_call_target="tpu_custom_call" | custom-call | tf_op jit(solution)/shard_map/finish/pallas_call | solution.py:633
